TPU v7x, 256 devices: a whole 4x4x8 slice. The times are simulated.
256 devices in a mesh: tile: 64 (over x_lo, y, z), member: 4 (over x_hi, core).
Axes of the slice: x: 4 (x_hi: 2, x_lo: 2; x = x_hi * 2 + x_lo), y: 4, z: 8, core: 2. Of those that a mesh axis runs over, the one named last changes fastest.
Arguments:
- states: bfloat16 [4, 16384, 512], P('member', 'tile'), may hold values from -105 to 105
- teacher: bfloat16 [16384, 512], P('tile'), may hold values from -6 to 6
- w_qkv: bfloat16 [512, 1536], replicated, may hold values from -0.25 to 0.25
- w_out: bfloat16 [512, 512], replicated, may hold values from -0.25 to 0.25
- gain: float32 [512], replicated, may hold values from 0.1 to 1.9
- bias: float32 [8, 64, 64], replicated, may hold values from -4 to 400
- neighbours: int32 [256, 9], P('tile'), may hold values from 0 to 255, as said below
- valid: int32 [256, 9], P('tile'), may hold values from 0 to 1, as said below
- orient: int32 [256, 9], P('tile'), may hold values from 0 to 3, as said below
Outputs:
- output: bfloat16 [4, 16384, 512], P('member', 'tile')
- d_states: bfloat16 [4, 16384, 512], P('member', 'tile')
- d_wqkv: float32 [512, 1536], P('tile', 'member')
- d_wout: float32 [512, 512], P('tile', 'member')
- d_gain: float32 [512], replicated
- d_bias: float32 [8, 64, 64], replicated
Inputs may be any that keep to these rules, and one draw needn't show every extreme that they name: `neighbours`: for a block in column c, slots 3 m, 3 m + 1 and 3 m + 2 name blocks of column c + m - 1, block = column * 4 + row; where c + m - 1 lies outside 0 to 64 - 1 (the window's open ends) these slots name the block itself; slot 4 names the block itself. `valid`: slot 4 is always 1; slots whose column lies outside the window are 0. `orient`: slot 4 is always 0.
All inputs are finite; a program needn't handle non-finite values.
Results may differ from a plain program's by a relative error of at most 0.008.
Values may be sent and summed in bfloat16 or wider, within the bound.
A program may use at most 128 MiB of HBM per device.

v0:
```python
import jax
import jax.numpy as jnp
from jax import lax
from jax.sharding import PartitionSpec as P

D = 512
HEADS = 8
HD = 64
SIDE = 8
PIX = 64
ROWS = 4
SLOTS = 9
COL_DEV = 1


EPS = 1e-06
NEG = -1e30
HIGH = lax.Precision.HIGHEST


def extended_2(cells, sides, width):
    for axis, dim in sides:
        count = lax.axis_size(axis)
        ends = count - 1
        head = lax.slice_in_dim(cells, 0, width, axis=dim)
        tail = lax.slice_in_dim(cells, cells.shape[dim] - width, cells.shape[dim], axis=dim)
        cells = jnp.concatenate(
            [
                lax.ppermute(tail, axis, [(i, (i + 1) % count) for i in range(ends)]),
                cells,
                lax.ppermute(head, axis, [((i + 1) % count, i) for i in range(ends)]),
            ],
            axis=dim,
        )
    return cells


def passed_along(value, axis, by):
    count = lax.axis_size(axis)
    pairs = [(i, i + by) for i in range(count) if 0 <= i + by < count]
    return lax.ppermute(value, axis, pairs)


def turn_onehot():
    position = jnp.arange(PIX, dtype=jnp.int32)
    upper = position // SIDE
    lower = position % SIDE
    tables = []
    for turn in range(4):
        tables.append(upper * SIDE + lower)
        upper, lower = (lower, SIDE - 1 - upper)
    table = jnp.stack(tables)
    return (table[:, :, None] == position[None, None, :]).astype(jnp.float32)


def probabilities(queries, keys_flat, inside, expander, turned_flat):
    scores = jnp.einsum(
        "gihd,gnhd->ghin", queries, keys_flat, preferred_element_type=jnp.float32
    ) * HD ** (-0.5)
    scores = scores + jnp.einsum("hic,gcn->ghin", turned_flat, expander, precision=HIGH)
    masked = jnp.where(inside, scores, NEG)
    highest = jnp.max(masked, axis=3, keepdims=True)
    weights = jnp.where(inside, jnp.exp(masked - highest), 0.0)
    return weights / jnp.sum(weights, axis=3, keepdims=True)


def shards(states, teacher, w_qkv, w_out, gain, bias, neighbours, valid, orient):
    inputs = states[0]
    n_rows = inputs.shape[0]
    blocks_here = neighbours.shape[0]
    cols_here = blocks_here // ROWS
    extended = blocks_here + 2 * ROWS
    rim_rows = ROWS * PIX
    n_tile = lax.axis_size("tile")
    n_member = lax.axis_size("member")
    first_column = lax.axis_index("tile") * COL_DEV
    columns_all = COL_DEV * n_tile
    near_column = jnp.mod(neighbours // ROWS - first_column + 1, columns_all)
    near_local = near_column * ROWS + neighbours % ROWS
    alive_flat = jnp.repeat(valid > 0, PIX, axis=1)
    inside = alive_flat[:, None, None, :]
    turn_pick = (orient[:, :, None] == jnp.arange(4, dtype=jnp.int32)[None, None, :]).astype(
        jnp.float32
    )
    identity = jnp.eye(PIX, dtype=jnp.float32)
    expander = jnp.einsum("gsk,jl->gkjsl", turn_pick, identity, precision=HIGH).reshape(
        blocks_here, 4 * PIX, SLOTS * PIX
    )
    onehot_turn = turn_onehot()
    turned = jnp.einsum("ail,kjl->kaij", bias, onehot_turn, precision=HIGH)
    turned_flat = jnp.transpose(turned, (1, 2, 0, 3)).reshape(HEADS, PIX, 4 * PIX)
    inputs32 = inputs.astype(jnp.float32)
    inverse = lax.rsqrt(jnp.mean(inputs32 * inputs32, axis=-1, keepdims=True) + EPS)
    normed = (inputs32 * inverse * gain).astype(jnp.bfloat16)
    projected = jnp.dot(normed, w_qkv, preferred_element_type=jnp.float32).astype(jnp.bfloat16)
    queries = projected[:, :D].reshape(blocks_here, PIX, HEADS, HD)
    keyval = projected[:, D:]
    keyval_ext = extended_2(keyval, (("tile", 0),), rim_rows)
    keyval_near = jnp.take(keyval_ext.reshape(extended, PIX, 2 * D), near_local, axis=0)
    keys_flat = keyval_near[..., :D].reshape(blocks_here, SLOTS * PIX, HEADS, HD)
    values_flat = keyval_near[..., D:].reshape(blocks_here, SLOTS * PIX, HEADS, HD)
    probs = probabilities(queries, keys_flat, inside, expander, turned_flat)
    probs_low = probs.astype(jnp.bfloat16)
    mixed = jnp.einsum(
        "ghin,gnhd->gihd", probs_low, values_flat, preferred_element_type=jnp.float32
    )
    mixed = mixed.astype(jnp.bfloat16).reshape(n_rows, D)
    output32 = inputs32 + jnp.dot(mixed, w_out, preferred_element_type=jnp.float32)
    d_output = (output32 - teacher.astype(jnp.float32)).astype(jnp.bfloat16)
    d_mixed = jnp.dot(d_output, w_out.T, preferred_element_type=jnp.float32).astype(jnp.bfloat16)
    d_mixed = d_mixed.reshape(blocks_here, PIX, HEADS, HD)
    d_probs = jnp.einsum(
        "gihd,gnhd->ghin", d_mixed, values_flat, preferred_element_type=jnp.float32
    )
    delta_sum = jnp.sum(probs * d_probs, axis=3, keepdims=True)
    d_scores = probs * (d_probs - delta_sum)
    d_scores_low = d_scores.astype(jnp.bfloat16)
    d_queries = jnp.einsum(
        "ghin,gnhd->gihd", d_scores_low, keys_flat, preferred_element_type=jnp.float32
    ) * HD ** (-0.5)
    d_queries = d_queries.astype(jnp.bfloat16).reshape(n_rows, D)
    d_keys = jnp.einsum(
        "ghin,gihd->gnhd", d_scores_low, queries, preferred_element_type=jnp.float32
    ) * HD ** (-0.5)
    d_values = jnp.einsum("ghin,gihd->gnhd", probs_low, d_mixed, preferred_element_type=jnp.float32)
    d_near = jnp.concatenate(
        [
            d_keys.reshape(blocks_here * SLOTS, PIX, D),
            d_values.reshape(blocks_here * SLOTS, PIX, D),
        ],
        axis=-1,
    )
    d_near = d_near.reshape(cols_here, ROWS, 3, 3, PIX * 2 * D)
    target_row = (neighbours % ROWS).reshape(cols_here, ROWS, 3, 3)
    row_onehot = (target_row[..., None] == jnp.arange(ROWS, dtype=jnp.int32)).astype(jnp.float32)
    per_group = jnp.einsum("cqmkt,cqmkx->mctx", row_onehot, d_near, precision=HIGH)
    d_columns = jnp.pad(per_group[0], ((0, 2), (0, 0), (0, 0)))
    d_columns = d_columns + jnp.pad(per_group[1], ((1, 1), (0, 0), (0, 0)))
    d_columns = d_columns + jnp.pad(per_group[2], ((2, 0), (0, 0), (0, 0)))
    d_extended = d_columns.reshape(extended * PIX, 2 * D)
    from_right = passed_along(d_extended[:rim_rows].astype(jnp.bfloat16), "tile", -1).astype(
        jnp.float32
    )
    from_left = passed_along(
        d_extended[extended * PIX - rim_rows :].astype(jnp.bfloat16), "tile", 1
    ).astype(jnp.float32)
    d_keyval = d_extended[rim_rows : extended * PIX - rim_rows]
    d_keyval = d_keyval.at[:rim_rows].add(from_left)
    d_keyval = d_keyval.at[n_rows - rim_rows :].add(from_right)
    d_proj = jnp.concatenate([d_queries, d_keyval.astype(jnp.bfloat16)], axis=-1)
    d_normed = jnp.dot(d_proj, w_qkv.T, preferred_element_type=jnp.float32)
    gain_term = jnp.sum(d_normed * inputs32 * inverse, axis=0)
    d_scaled = d_normed * gain
    d_inputs = (
        d_output.astype(jnp.float32)
        + inverse * d_scaled
        - inputs32
        * inverse
        * inverse
        * inverse
        * jnp.mean(d_scaled * inputs32, axis=-1, keepdims=True)
    )
    d_table = jnp.einsum("ghin,gcn->hic", d_scores, expander, precision=HIGH)
    d_turned = jnp.transpose(d_table.reshape(HEADS, PIX, 4, PIX), (2, 0, 1, 3))
    bias_term = jnp.einsum("khij,kjl->hil", d_turned, onehot_turn, precision=HIGH)
    gain_total, bias_total = lax.psum((gain_term, bias_term), ("tile", "member"))
    proj_cols = 3 * D // n_member
    out_cols = D // n_member
    proj_part = jnp.einsum("rd,re->de", normed, d_proj, preferred_element_type=jnp.float32).reshape(
        D // n_tile * lax.axis_size("tile"), n_member, proj_cols
    )
    out_part = jnp.einsum("rd,re->de", mixed, d_output, preferred_element_type=jnp.float32).reshape(
        D // n_tile * lax.axis_size("tile"), n_member, out_cols
    )
    tile_shares = lax.psum_scatter(
        jnp.concatenate([proj_part, out_part], axis=2), "tile", scatter_dimension=0, tiled=True
    )
    summed = lax.psum_scatter(
        tile_shares.astype(jnp.bfloat16), "member", scatter_dimension=1, tiled=True
    ).astype(jnp.float32)
    d_wqkv = summed[:, 0, :proj_cols]
    d_wout = summed[:, 0, proj_cols:]
    return (
        output32.astype(jnp.bfloat16)[None],
        d_inputs.astype(jnp.bfloat16)[None],
        d_wqkv,
        d_wout,
        gain_total,
        bias_total,
    )


def solution(mesh):
    return jax.shard_map(
        shards,
        mesh=mesh,
        in_specs=(
            P("member", "tile", None),
            P("tile", None),
            P(),
            P(),
            P(),
            P(),
            P("tile", None),
            P("tile", None),
            P("tile", None),
        ),
        out_specs=(
            P("member", "tile", None),
            P("member", "tile", None),
            P("tile", "member"),
            P("tile", "member"),
            P(),
            P(),
        ),
        check_vma=False,
    )
```

profile of v0, /device:TPU:1, one launch (start us, length us, event | category | flops | bytes accessed | tf_op | source)
XLA Modules:
  0.0 891.3 jit_solution(7698025459026587892)
XLA Ops:
  12.5 5.8 collective-permute-start
  18.4 3.3 multiply_bitcast_fusion.1
  21.8 5.4 reshape.271
  27.2 5.5 reshape.250
  39.2 3.2 copy.107
  45.1 4.5 gather_fusion
  49.7 2.8 broadcast_select_fusion
  52.5 2.7 fusion.72
  55.3 7.0 reshape.249
  62.3 6.3 copy.89
  68.5 7.0 reshape.247
  75.6 18.6 %copy.91 = bf16[4,576,8,64]{1,3,2,0:T(8,128)(2,1)} copy(bf16[4,576,8,64]{3,2,1,0:T(8,128)(2,1)} %reshape.247) | data formatting | bytes 4718592 | tf_op jit(solution)/shard_map/reshape | solution.py:101
  94.3 2.8 fusion.76
  97.1 5.5 fusion.4
  118.1 4.8 multiply_reduce_fusion
  122.9 3.3 convolution_bitcast_fusion.1
  126.2 2.8 fusion.8
  130.8 3.1 multiply_bitcast_fusion
  136.4 8.1 copy.101
  144.6 9.0 %reshape.256 = f32[36,64,512]{2,1,0:T(8,128)} reshape(f32[4,576,8,64]{3,2,1,0:T(8,128)} %copy.101) | data formatting | bytes 9437184 | tf_op jit(solution)/shard_map/reshape | solution.py:129
  153.5 8.1 copy.99
  161.7 9.0 %reshape.255 = f32[36,64,512]{2,1,0:T(8,128)} reshape(f32[4,576,8,64]{3,2,1,0:T(8,128)} %copy.99) | data formatting | bytes 9437184 | tf_op jit(solution)/shard_map/reshape | solution.py:128
  170.6 9.1 %pad_maximum_fusion = f32[36,64,1024]{2,1,0:T(8,128)} fusion(f32[36,64,512]{2,1,0:T(8,128)} %reshape.256, f32[36,64,512]{2,1,0:T(8,128)} %reshape.255), kind=kLoop, calls=%fused_computation.3 | loop fusion | flops 2359296 | bytes 18874368 | tf_op jit(solution)/shard_map/concatenate | solution.py:126
  179.7 14.1 %reshape.257 = f32[4,3,3,65536]{3,2,1,0:T(4,128)} reshape(f32[36,64,1024]{2,1,0:T(8,128)} %pad_maximum_fusion) | data formatting | bytes 18874368 | tf_op jit(solution)/shard_map/reshape.68
  193.8 20.7 %convolution_bitcast_fusion = f32[3,4,65536]{2,1,0:T(4,128)S(1)} fusion(f32[4,3,3,65536]{3,2,1,0:T(4,128)} %reshape.257, s32[4,3,3]{0,2,1:T(4,128)S(1)} %copy.97), kind=kOutput, calls=%fused_computation.2 | convolution fusion | flops 113246352 | bytes 12583056 | tf_op jit(solution)/shard_map/cqmkt,cqmkx->mctx/dot_general | solution.py:136
  215.2 2.9 fusion.71
  222.2 4.8 collective-permute-start.2
  233.6 11.8 %fusion.10 = f32[4,8,64,64]{3,2,0,1:T(8,128)} fusion(f32[4,64,4,576]{3,1,0,2:T(8,128)} %bitcast.155, f32[4,8,64,576,1]{3,2,1,0,4:T(8,128)} %get-tuple-element.70), kind=kOutput, calls=%fused_computation.26 | convolution fusion | flops 3623878656 | bytes 7602176 | tf_op jit(solution)/shard_map/ghin,gcn->hic/dot_general | solution.py:163
  255.3 5.4 copy.105
  260.7 308.8 %all-reduce.7 = bf16[512,4,512]{2,1,0:T(4,128)(2,1)} all-reduce(f32[512,4,512]{2,1,0:T(4,128)} %copy.105), channel_id=2, replica_groups=mesh['tile'=64,'member'=4] {'tile'}, use_global_device_ids=true, to_apply=%region_5.6.clone | all-reduce | flops 1048576 | bytes 6291456
  574.3 133.7 %psum.14 = f32[512]{0:T(512)} all-reduce(f32[512]{0:T(512)S(1)} %get-tuple-element.64), channel_id=1, replica_groups=mesh['tile'=64,'member'=4] {'tile','member'}, use_global_device_ids=true, to_apply=%region_8.9 | all-reduce | flops 512 | bytes 4096 | tf_op jit(solution)/shard_map/psum | solution.py:166
  710.9 171.1 %all-reduce.6.cloned.1.call-done = f32[8,64,64]{2,1,0:T(8,128)} async-done(((f32[8,64,64]{2,1,0:T(8,128)}), f32[8,64,64]{2,1,0:T(8,128)}) %all-reduce.6.cloned.1.call-update) | async-done | bytes 131088 | tf_op jit(solution)/shard_map/psum | solution.py:166
  (126 shorter events, 63.4 us)
Async XLA Ops:
  8.0 1.5 copy-start
  8.0 10.3 %copy-start.21 = (s32[4,9]{1,0:T(4,128)S(1)}, s32[4,9]{1,0:T(4,128)}, u32[]{:S(2)}) copy-start(s32[4,9]{1,0:T(4,128)} %param.24) | copy-start | bytes 436
  8.0 10.3 %copy-start.19 = (s32[4,9]{1,0:T(4,128)S(1)}, s32[4,9]{1,0:T(4,128)}, u32[]{:S(2)}) copy-start(s32[4,9]{1,0:T(4,128)} %param.23) | copy-start | bytes 436
  8.0 10.3 %copy-start.20 = (s32[4,9]{1,0:T(4,128)S(1)}, s32[4,9]{1,0:T(4,128)}, u32[]{:S(2)}) copy-start(s32[4,9]{1,0:T(4,128)} %param.25) | copy-start | bytes 436
  8.0 701.0 %reduce-scatter.2.cloned.1.call-start = ((), (), s32[]{:S(2)}) async-start(), calls=%async_computation.1 | async-start | bytes 40960 | tf_op jit(solution)/shard_map/reduce_scatter | solution.py:178
  11.1 10.7 %copy-start.9 = (bf16[256,1536]{1,0:T(8,128)(2,1)}, bf16[256,1536]{1,0:T(8,128)(2,1)S(1)}, u32[]{:S(2)}) copy-start(bf16[256,1536]{1,0:T(8,128)(2,1)S(1)} %convolution_convert_fusion) | copy-start | bytes 2359300
  11.1 16.1 %copy-start.15 = (bf16[256,1024]{1,0:T(8,128)(2,1)}, bf16[256,1024]{1,0:T(8,128)(2,1)S(1)}, u32[]{:S(2)}) copy-start(bf16[256,1024]{1,0:T(8,128)(2,1)S(1)} %slice.87) | copy-start | bytes 1572868
  11.2 32.5 %collective-permute-start.1 = (bf16[256,1024]{1,0:T(8,128)(2,1)S(1)}, bf16[256,1024]{1,0:T(8,128)(2,1)}, u32[]{:S(2)}, u32[]{:S(2)}) collective-permute-start(bf16[256,1024]{1,0:T(8,128)(2,1)S(1)} %slice.87), channel_id=1, source_target_pairs={{4,0},{8,4},{12,8},{16,12},{20,16},{24,20},{28,24},{32,28},{36,32}... | collective-permute-start | bytes 1572872 | tf_op jit(solution)/shard_map/ppermute | solution.py:31
  12.5 31.2 %collective-permute-start = (bf16[256,1024]{1,0:T(8,128)(2,1)S(1)}, bf16[256,1024]{1,0:T(8,128)(2,1)}, u32[]{:S(2)}, u32[]{:S(2)}) collective-permute-start(bf16[256,1024]{1,0:T(8,128)(2,1)S(1)} %slice.87), channel_id=1, source_target_pairs={{0,4},{4,8},{8,12},{12,16},{16,20},{20,24},{24,28},{28,32},{32,36}... | collective-permute-start | bytes 1572872 | tf_op jit(solution)/shard_map/ppermute | solution.py:29
  27.2 5.9 slice-start.2
  27.2 7.4 copy-start.17
  36.5 5.8 copy-start.23
  75.6 18.6 %copy-start.4 = (bf16[4,64,8,64]{1,3,2,0:T(8,128)(2,1)S(1)}, bf16[4,64,8,64]{1,3,2,0:T(8,128)(2,1)}, u32[]{:S(2)}) copy-start(bf16[4,64,8,64]{1,3,2,0:T(8,128)(2,1)} %copy.98) | copy-start | bytes 786436
  94.2 2.8 copy-start.3
  94.2 2.8 copy-start.11
  102.5 3.9 copy-start.10
  104.1 2.3 copy-start.2
  106.4 5.3 copy-start.5
  106.4 5.3 copy-start.14
  113.7 0.7 copy-start.6
  115.9 7.0 slice-start
  118.1 4.8 slice-start.1
  118.1 4.8 copy-start.16
  126.2 2.8 copy-start.1
  130.8 3.1 copy-start.7
  220.9 24.5 %collective-permute-start.3 = (bf16[256,1024]{1,0:T(8,128)(2,1)}, bf16[256,1024]{1,0:T(8,128)(2,1)}, u32[]{:S(2)}, u32[]{:S(2)}) collective-permute-start(bf16[256,1024]{1,0:T(8,128)(2,1)} %convert_element_type.106), channel_id=1, source_target_pairs={{4,0},{8,4},{12,8},{16,12},{20,16},{24,20},{28,24},{32,28},{36,32}... | collective-permute-start | bytes 1572872 | tf_op jit(solution)/shard_map/ppermute | solution.py:41
  222.2 23.2 %collective-permute-start.2 = (bf16[256,1024]{1,0:T(8,128)(2,1)}, bf16[256,1024]{1,0:T(8,128)(2,1)}, u32[]{:S(2)}, u32[]{:S(2)}) collective-permute-start(bf16[256,1024]{1,0:T(8,128)(2,1)} %convert_element_type.104), channel_id=1, source_target_pairs={{0,4},{4,8},{8,12},{12,16},{16,20},{20,24},{24,28},{28,32},{32,36}... | collective-permute-start | bytes 1572872 | tf_op jit(solution)/shard_map/ppermute | solution.py:41
  245.4 5.6 copy-start.18
  246.8 0.8 copy-start.12
  248.6 4.2 copy-start.8
  260.7 312.9 %copy-start.13 = (bf16[256,1024]{1,0:T(8,128)(2,1)S(1)}, bf16[256,1024]{1,0:T(8,128)(2,1)}, u32[]{:S(2)}) copy-start(bf16[256,1024]{1,0:T(8,128)(2,1)} %copy-done.12) | copy-start | bytes 1572868
  571.0 311.0 %all-reduce.6.cloned.1.call-start = ((), (), s32[]{:S(2)}) async-start(), calls=%async_computation.2 | async-start | bytes 524288 | tf_op jit(solution)/shard_map/psum | solution.py:166
  (1 other events, 0.7 us)
Sparse Core Ops, SparseCore 0:
  571.1 85.5 reduce-scatter.1
Sparse Core Ops, SparseCore 1:
  578.3 303.6 all-reduce.5
where the time goes:
time: 896 us; the launch traced here: 891 us
  blocking collectives  443 us (49%)
  waiting for transfers between devices  171 us (19%)
  local copies, waits for them, and re-layouts  148 us (17%)
  matrix products  67.5 us (8%)
  other arithmetic  31.9 us (4%)
  between operations  16.8 us (2%)
  starting transfers between devices  13.2 us (1%)
    unnamed x1, blocking collectives  309 us
    psum x1, waiting for transfers between devices, shards(): lax.psum((gain_term, bias_term), ('tile', 'member'))  171 us
    psum x1, blocking collectives, shards(): lax.psum((gain_term, bias_term), ('tile', 'member'))  134 us
    reshape x2, local copies, waits for them, and re-layouts, shards(): keyval_near[..., D:].reshape(blocks_here, SLOTS * PIX, HEADS, HD)  25.7 us
    dot_general x1, matrix products, shards(): jnp.einsum('cqmkt,cqmkx->mctx', row_onehot, d_near, precision=HIGH)  20.7 us
  transfers between devices with their start and end apart: 6, of which 1 were waited for; matrix products, arithmetic and copies ran while one was open for 6% of the time, Pallas kernels for 0%

commit v1 on v0

v1 whole, which is shorter than its diff:
```python
import functools

import jax
import jax.numpy as jnp
from jax import lax
from jax.experimental import pallas as pl
from jax.experimental.pallas import tpu as pltpu
from jax.sharding import PartitionSpec as P

D = 512
HEADS = 8
HD = 64
PIX = 64
ROWS = 4
SLOTS = 9
HALF = 256
EPS = 1e-06
NEG = -1e30
MESH = pl.DeviceIdType.MESH
F32 = jnp.float32
BF16 = jnp.bfloat16

NX, NY, NZ, NXL = 4, 4, 8, 2
N_TILE = NXL * NY * NZ

NN = (((1,), (0,)), ((), ()))
NT = (((1,), (1,)), ((), ()))
TN = (((0,), (0,)), ((), ()))


def mm(a, b, dims=NN):
    return lax.dot_general(a, b, dims, preferred_element_type=F32)


def kernel(
    x_ref, teacher_ref, wqkv_ref, wout_ref, gain_ref, bias_ref, near_ref, valid_ref, orient_ref,
    out_ref, dst_ref, dwqkv_ref, dwout_ref, dgain_ref, dbias_ref,
    xh, nb, kbuf, vbuf, tb, oh, qb, kg, vg, sref, pb, rinv, mixed, dmix, dout, dsb, dq,
    qd, md, dcat, pcat, dkv, esend, erecv, turns,
    g0, r0, s1, ra1, rb1, a1, b1, ra2, rb2, c3, rz,
    u0, ruz, w0, ruc, rux, ruy, fz,
    send, recv,
):
    tile = lax.axis_index("tile")
    member = lax.axis_index("member")
    z = lax.rem(tile, NZ)
    y = lax.rem(tile // NZ, NY)
    x = (member // 2) * NXL + tile // (NZ * NY)
    core = lax.rem(member, 2)

    def at(x_=None, y_=None, z_=None, core_=None):
        x_ = x if x_ is None else x_
        y_ = y if y_ is None else y_
        z_ = z if z_ is None else z_
        core_ = core if core_ is None else core_
        return (lax.rem(x_, NXL) * NY + y_) * NZ + z_, (x_ // NXL) * 2 + core_

    right = (lax.rem(tile + 1, N_TILE), member)
    left = (lax.rem(tile + N_TILE - 1, N_TILE), member)
    sibling = at(core_=1 - core)
    xs = [lax.rem(x + o, NX) for o in range(1, NX)]
    ys = [lax.rem(y + o, NY) for o in range(1, NY)]
    zs = [lax.rem(z + o, NZ) for o in range(1, NZ)]
    peers = [left, right, sibling]
    peers += [at(x_=v) for v in xs] + [at(y_=v) for v in ys] + [at(z_=v) for v in zs]

    started = []

    def push(src, dst, to):
        n = len(started)
        copy = pltpu.make_async_remote_copy(
            src_ref=src, dst_ref=dst, send_sem=send.at[n], recv_sem=recv.at[n],
            device_id=to, device_id_type=MESH,
        )
        copy.start()
        started.append(copy)
        return copy

    barrier = pltpu.get_barrier_semaphore()
    for p in peers:
        pl.semaphore_signal(barrier, inc=1, device_id=p, device_id_type=MESH)
    pl.semaphore_wait(barrier, len(peers))

    to_right = push(x_ref, xh.at[0], right)
    to_left = push(x_ref, xh.at[1], left)

    gain = gain_ref[...]

    def inverse_of(v32):
        return lax.rsqrt(jnp.mean(v32 * v32, axis=-1, keepdims=True) + EPS)

    def normalised(v):
        v32 = v.astype(F32)
        return (v32 * inverse_of(v32) * gain).astype(BF16)

    nb[HALF:2 * HALF, :] = normalised(x_ref[...])
    own = nb[HALF:2 * HALF, :]
    qb[...] = (mm(own, wqkv_ref[:, :D]).astype(BF16) * 0.125).astype(BF16)

    def keys_values(m):
        rows = nb[m * HALF:(m + 1) * HALF, :]
        kbuf[m * ROWS:(m + 1) * ROWS] = mm(rows, wqkv_ref[:, D:2 * D]).astype(BF16).reshape(ROWS, PIX, D)
        vbuf[m * ROWS:(m + 1) * ROWS] = mm(rows, wqkv_ref[:, 2 * D:]).astype(BF16).reshape(ROWS, PIX, D)

    keys_values(1)

    j = lax.broadcasted_iota(jnp.int32, (PIX, 128), 0)
    l = lax.broadcasted_iota(jnp.int32, (PIX, 128), 1)
    u, w = j // 8, j % 8
    for o in range(4):
        oh[o] = jnp.where(l == u * 8 + w, 1.0, 0.0).astype(BF16)
        pick = jnp.where(l[:, :PIX] == (u * 8 + w)[:, :PIX], 1.0, 0.0)
        tb[o] = lax.dot_general(
            pick, bias_ref[...], NT, precision=lax.Precision.HIGHEST, preferred_element_type=F32
        )
        u, w = w, 7 - u
    tb[4] = jnp.full((PIX, D), NEG, F32)

    head_row = lax.broadcasted_iota(jnp.int32, (HALF, HALF), 0) // HD
    head_lane = lax.broadcasted_iota(jnp.int32, (HALF, HALF), 1) // HD
    same_head = jnp.where(head_row == head_lane, 1.0, 0.0).astype(BF16)
    lane_head = lax.broadcasted_iota(jnp.int32, (PIX, HALF), 1) // HD

    def block_diagonal(v):
        return jnp.concatenate([v] * 4, axis=0) * same_head

    def diagonal(v):
        out = v[:PIX]
        for a in range(1, 4):
            out = jnp.where(lane_head == a, v[a * PIX:(a + 1) * PIX], out)
        return out

    groups = [slice(0, HALF), slice(HALF, D)]

    to_right.wait_recv()
    to_left.wait_recv()
    nb[:HALF, :] = normalised(xh[0])
    nb[2 * HALF:, :] = normalised(xh[1])
    keys_values(0)
    keys_values(2)

    for b in range(ROWS):
        for s in range(SLOTS):
            at_block = (s // 3) * ROWS + lax.rem(near_ref[b, s], ROWS)
            kg[b, s * PIX:(s + 1) * PIX, :] = kbuf[at_block]
            vg[b, s * PIX:(s + 1) * PIX, :] = vbuf[at_block]
        tables = [jnp.where(valid_ref[b, s] > 0, orient_ref[b, s], 4) for s in range(SLOTS)]
        for g, lanes in enumerate(groups):
            diag = block_diagonal(qb[b * PIX:(b + 1) * PIX, lanes])
            qd[g, b * HALF:(b + 1) * HALF, :] = diag
            scores = mm(kg[b, :, lanes], diag, NT)
            top = None
            for s in range(SLOTS):
                piece = scores[s * PIX:(s + 1) * PIX] + tb[tables[s], :, lanes]
                sref[b, s * PIX:(s + 1) * PIX, lanes] = piece
                top = piece if top is None else jnp.maximum(top, piece)
            top = jnp.max(top, axis=0, keepdims=True)
            total = None
            for s in range(SLOTS):
                piece = jnp.exp(sref[b, s * PIX:(s + 1) * PIX, lanes] - top)
                sref[b, s * PIX:(s + 1) * PIX, lanes] = piece
                total = piece if total is None else total + piece
            share = 1.0 / jnp.sum(total, axis=0, keepdims=True)
            rinv[b, :, lanes] = share
            for s in range(SLOTS):
                piece = sref[b, s * PIX:(s + 1) * PIX, lanes] * share
                pb[b, s, :, lanes] = piece.astype(BF16)
            probs = pb[b, 0:SLOTS, :, lanes].reshape(SLOTS * PIX, HALF)
            mixed[b * PIX:(b + 1) * PIX, lanes] = diagonal(mm(probs, vg[b, :, lanes], TN)).astype(BF16)
        pb[b, SLOTS] = jnp.zeros((PIX, D), BF16)
        dsb[b, SLOTS] = jnp.zeros((PIX, D), BF16)

    out32 = x_ref[...].astype(F32) + mm(mixed[...], wout_ref[...])
    out_ref[...] = out32.astype(BF16)
    dout[...] = (out32 - teacher_ref[...].astype(F32)).astype(BF16)
    dmix[...] = mm(dout[...], wout_ref[...], NT).astype(BF16)

    for b in range(ROWS):
        for g, lanes in enumerate(groups):
            diag = block_diagonal(dmix[b * PIX:(b + 1) * PIX, lanes])
            md[g, b * HALF:(b + 1) * HALF, :] = diag
            dprobs = mm(vg[b, :, lanes], diag, NT)
            share = rinv[b, :, lanes]
            total = None
            for s in range(SLOTS):
                piece = sref[b, s * PIX:(s + 1) * PIX, lanes] * dprobs[s * PIX:(s + 1) * PIX]
                total = piece if total is None else total + piece
            delta = jnp.sum(total, axis=0, keepdims=True) * share
            for s in range(SLOTS):
                piece = sref[b, s * PIX:(s + 1) * PIX, lanes] * share
                piece = piece * (dprobs[s * PIX:(s + 1) * PIX] - delta)
                dsb[b, s, :, lanes] = piece.astype(BF16)
            dscores = dsb[b, 0:SLOTS, :, lanes].reshape(SLOTS * PIX, HALF)
            dq[b * PIX:(b + 1) * PIX, lanes] = (diagonal(mm(dscores, kg[b, :, lanes], TN)) * 0.125).astype(BF16)
        rows = [lax.rem(near_ref[b, s], ROWS) for s in range(SLOTS)]
        for m in range(3):
            for t in range(ROWS):
                slots = [jnp.where(rows[3 * m + k] == t, 3 * m + k, SLOTS) for k in range(3)]
                here = slice((m * ROWS + t) * PIX, (m * ROWS + t + 1) * PIX)
                ds = dsb[b, slots[0]] + dsb[b, slots[1]] + dsb[b, slots[2]]
                ps = pb[b, slots[0]] + pb[b, slots[1]] + pb[b, slots[2]]
                for g, lanes in enumerate(groups):
                    dcat[g, here, b * HALF:(b + 1) * HALF] = ds[:, lanes]
                    pcat[g, here, b * HALF:(b + 1) * HALF] = ps[:, lanes]

    for g in range(2):
        dkv[:, g * HALF:(g + 1) * HALF] = mm(dcat[g], qd[g]).astype(BF16)
        dkv[:, D + g * HALF:D + (g + 1) * HALF] = mm(pcat[g], md[g]).astype(BF16)

    def share_out(value, m, offset):
        low = value.astype(BF16)
        for xl in range(NXL):
            for yy in range(NY):
                for zh in range(2):
                    fb = (xl * NY + yy) * 2 + zh
                    g0[m % 2, zh, (m // 2) * NXL + xl, yy, :, offset:offset + low.shape[1]] = low[fb * 32:(fb + 1) * 32]

    for m in range(4):
        for lo in range(m * 384, m * 384 + 384, 128):
            if lo < D:
                value = mm(own, dq[:, lo:lo + 128], TN)
            else:
                value = mm(nb[...], dkv[:, lo - D:lo - D + 128], TN)
            share_out(value, m, lo - m * 384)
        share_out(mm(mixed[...], dout[:, m * 128:(m + 1) * 128], TN), m, 384)

    g_core = push(g0.at[1 - core], r0, sibling)

    wkv = wqkv_ref[:, D:]

    def scaled(v):
        v32 = v.astype(F32)
        return v32 * inverse_of(v32)

    def by_eight(v):
        return jnp.sum(v.reshape(HALF // 8, 8, D), axis=0)

    edge = mm(dkv[:HALF, :], wkv, NT)
    esend[0] = edge.astype(BF16)
    e_left = push(esend.at[0], erecv.at[0], left)
    gain8 = by_eight(edge * scaled(xh[0]))
    edge = mm(dkv[2 * HALF:, :], wkv, NT)
    esend[1] = edge.astype(BF16)
    e_right = push(esend.at[1], erecv.at[1], right)
    gain8 = gain8 + by_eight(edge * scaled(xh[1]))
    dnorm = mm(dkv[HALF:2 * HALF, :], wkv, NT) + mm(dq[...], wqkv_ref[:, :D], NT)
    gain8 = gain8 + by_eight(dnorm * scaled(x_ref[...]))

    dbias = None
    for b in range(ROWS):
        for s in range(SLOTS):
            turns[s * PIX:(s + 1) * PIX, :] = oh[orient_ref[b, s]]
        part = mm(turns[...], dsb[b, 0:SLOTS].reshape(SLOTS * PIX, D), TN)[:PIX]
        dbias = part if dbias is None else dbias + part

    for i in range(NZ):
        u0[i, :, :D] = dbias[i * 8:(i + 1) * 8]
        u0[i, :, D:] = gain8[:, i * 128:(i + 1) * 128] if i < 4 else jnp.zeros((8, 128), F32)
    u_z = [push(u0.at[v], ruz.at[o], at(z_=v)) for o, v in enumerate(zs)]

    g_core.wait_recv()
    for zh in range(2):
        for xx in range(NX):
            s1[zh, xx] = (g0[core, zh, xx].astype(F32) + r0[zh, xx].astype(F32)).astype(BF16)
    a_x = [push(s1.at[0, v], ra1.at[o], at(x_=v)) for o, v in enumerate(xs)]
    b_y = [push(s1.at[1, :, v], rb1.at[o], at(y_=v)) for o, v in enumerate(ys)]

    for c in u_z:
        c.wait_recv()
    total = u0[z]
    for o in range(NZ - 1):
        total = total + ruz[o]
    w0[...] = total
    u_core = push(w0, ruc, sibling)
    u_core.wait_recv()
    rux[x] = w0[...] + ruc[...]
    u_x = [push(rux.at[x], rux.at[x], at(x_=v)) for v in xs]

    for c in a_x + b_y:
        c.wait_recv()
    a1[...] = (
        s1[0, x].astype(F32) + ra1[0].astype(F32) + ra1[1].astype(F32) + ra1[2].astype(F32)
    ).astype(BF16)
    for xx in range(NX):
        b1[xx] = (
            s1[1, xx, y].astype(F32) + rb1[0, xx].astype(F32) + rb1[1, xx].astype(F32) + rb1[2, xx].astype(F32)
        ).astype(BF16)
    a_y = [push(a1.at[v], ra2.at[o], at(y_=v)) for o, v in enumerate(ys)]
    b_x = [push(b1.at[v], rb2.at[o], at(x_=v)) for o, v in enumerate(xs)]

    for c in u_x:
        c.wait_recv()
    ruy[y] = rux[0] + rux[1] + rux[2] + rux[3]
    u_y = [push(ruy.at[y], ruy.at[y], at(y_=v)) for v in ys]

    for c in a_y + b_x:
        c.wait_recv()
    ca = a1[y].astype(F32) + ra2[0].astype(F32) + ra2[1].astype(F32) + ra2[2].astype(F32)
    cb = b1[x].astype(F32) + rb2[0].astype(F32) + rb2[1].astype(F32) + rb2[2].astype(F32)
    for i in range(NZ):
        part = (ca if i < 4 else cb)[(i % 4) * 8:(i % 4) * 8 + 8]
        c3[i] = jnp.concatenate([part[:, :HALF], part[:, HALF:]], axis=0).astype(BF16)
    c_z = [push(c3.at[v], rz.at[o], at(z_=v)) for o, v in enumerate(zs)]

    for c in u_y:
        c.wait_recv()
    fz[z] = ruy[0] + ruy[1] + ruy[2] + ruy[3]
    f_z = [push(fz.at[z], fz.at[z], at(z_=v)) for v in zs]

    e_left.wait_recv()
    e_right.wait_recv()
    dnorm = dnorm + erecv[0].astype(F32) + erecv[1].astype(F32)
    x32 = x_ref[...].astype(F32)
    inverse = inverse_of(x32)
    dscaled = dnorm * gain
    dst_ref[...] = (
        dout[...].astype(F32)
        + inverse * dscaled
        - x32 * (inverse * inverse * inverse * jnp.mean(dscaled * x32, axis=-1, keepdims=True))
    ).astype(BF16)

    for c in c_z:
        c.wait_recv()
    final = c3[z].astype(F32)
    for o in range(NZ - 1):
        final = final + rz[o].astype(F32)
    dwqkv_ref[:, :HALF] = final[:8]
    dwqkv_ref[:, HALF:] = final[8:, :128]
    dwout_ref[...] = final[8:, 128:]

    for c in f_z:
        c.wait_recv()
    dbias_ref[...] = fz[:, :, :D].reshape(PIX, D).T
    for i in range(4):
        dgain_ref[:, i * 128:(i + 1) * 128] = jnp.sum(fz[i, :, D:], axis=0, keepdims=True)

    for c in started:
        c.wait_send()


N_COPIES = 2 + 1 + 2 + 7 + 6 + 1 + 3 + 6 + 3 + 7 + 7


def scratch():
    def v(*shape, kind=BF16):
        return pltpu.VMEM(shape, kind)

    return [
        v(2, HALF, D), v(3 * HALF, D), v(12, PIX, D), v(12, PIX, D), v(5, PIX, D, kind=F32), v(4, PIX, 128),
        v(HALF, D), v(ROWS, SLOTS * PIX, D), v(ROWS, SLOTS * PIX, D), v(ROWS, SLOTS * PIX, D, kind=F32),
        v(ROWS, SLOTS + 1, PIX, D), v(ROWS, 1, D, kind=F32), v(HALF, D), v(HALF, D), v(HALF, D),
        v(ROWS, SLOTS + 1, PIX, D), v(HALF, D),
        v(2, ROWS * HALF, HALF), v(2, ROWS * HALF, HALF), v(2, 12 * PIX, ROWS * HALF), v(2, 12 * PIX, ROWS * HALF),
        v(3 * HALF, 2 * D), v(2, HALF, D), v(2, HALF, D), v(SLOTS * PIX, 128),
        v(2, 2, NX, NY, 32, D), v(2, NX, NY, 32, D), v(2, NX, NY, 32, D),
        v(NX - 1, NY, 32, D), v(NY - 1, NX, 32, D), v(NY, 32, D), v(NX, 32, D),
        v(NY - 1, 32, D), v(NX - 1, 32, D), v(NZ, 16, HALF), v(NZ - 1, 16, HALF),
        v(NZ, 8, D + 128, kind=F32), v(NZ - 1, 8, D + 128, kind=F32), v(8, D + 128, kind=F32), v(8, D + 128, kind=F32),
        v(NX, 8, D + 128, kind=F32), v(NY, 8, D + 128, kind=F32), v(NZ, 8, D + 128, kind=F32),
        pltpu.SemaphoreType.DMA((N_COPIES,)), pltpu.SemaphoreType.DMA((N_COPIES,)),
    ]


def shards(states, teacher, w_qkv, w_out, gain, bias, neighbours, valid, orient):
    vmem = pl.BlockSpec(memory_space=pltpu.VMEM)
    smem = pl.BlockSpec(memory_space=pltpu.SMEM)
    output, d_states, d_wqkv, d_wout, d_gain, d_bias = pl.pallas_call(
        kernel,
        out_shape=[
            jax.ShapeDtypeStruct((HALF, D), BF16),
            jax.ShapeDtypeStruct((HALF, D), BF16),
            jax.ShapeDtypeStruct((8, 384), F32),
            jax.ShapeDtypeStruct((8, 128), F32),
            jax.ShapeDtypeStruct((1, D), F32),
            jax.ShapeDtypeStruct((HEADS * PIX, PIX), F32),
        ],
        in_specs=[vmem] * 6 + [smem] * 3,
        out_specs=[vmem] * 6,
        scratch_shapes=scratch(),
        compiler_params=pltpu.CompilerParams(
            collective_id=0, has_side_effects=True, vmem_limit_bytes=60 * 2**20
        ),
    )(
        states[0], teacher, w_qkv, w_out, gain.reshape(1, D), bias.reshape(HEADS * PIX, PIX),
        neighbours, valid, orient,
    )
    return output[None], d_states[None], d_wqkv, d_wout, d_gain[0], d_bias.reshape(HEADS, PIX, PIX)


def solution(mesh):
    return jax.shard_map(
        shards,
        mesh=mesh,
        in_specs=(
            P("member", "tile", None), P("tile", None), P(), P(), P(), P(),
            P("tile", None), P("tile", None), P("tile", None),
        ),
        out_specs=(
            P("member", "tile", None), P("member", "tile", None), P("tile", "member"), P("tile", "member"), P(), P(),
        ),
        check_vma=False,
    )
```

time: 896 us -> 70.5 us (0.08)
  blocking collectives: 443 us -> 0 us
  waiting for transfers between devices: 171 us -> 0 us
  local copies, waits for them, and re-layouts: 148 us -> 8.82 us
  matrix products: 67.5 us -> 0 us
  Pallas kernels: 0 us -> 60.7 us
  other arithmetic: 31.9 us -> 0 us
  between operations: 16.8 us -> 0.65 us
  starting transfers between devices: 13.2 us -> 0 us
    unnamed x1 -> x0, blocking collectives: 309 us -> none
    psum x1 -> x0, waiting for transfers between devices: 171 us -> none  [shards(): lax.psum((gain_term, bias_term), ('tile', 'member'))]
    psum x1 -> x0, blocking collectives: 134 us -> none  [shards(): lax.psum((gain_term, bias_term), ('tile', 'member'))]
    reshape x16 -> x0, local copies, waits for them, and re-layouts: 77.5 us -> none  [the longest x2 25.7 us: shards(): keyval_near[..., D:].reshape(blocks_here, SLOTS * PIX, HEADS, HD)]
    dot_general x17 -> x0, matrix products: 67.5 us -> none  [the longest x1 20.7 us: shards(): jnp.einsum('cqmkt,cqmkx->mctx', row_onehot, d_near, precision=HIGH)]
    pallas_call x0 -> x1, Pallas kernels: none -> 60.7 us  [shards(): pl.pallas_call(kernel, out_shape=[jax.ShapeDtypeStruct((HALF, D), BF16),...]
    another operation x1 -> x0, local copies, waits for them, and re-layouts: 14.1 us -> none
    ppermute x4 -> x0, starting transfers between devices: 13.2 us -> none  [the longest x2 6.08 us: passed_along(): return lax.ppermute(value, axis, pairs)]
  transfers between devices with their start and end apart: 6 -> 0, of which waited for: 1 -> 0; matrix products, arithmetic and copies ran while one was open for 6% -> 0% of each run, Pallas kernels for 0% -> 0%
where the time goes in v1:
time: 70.5 us; the launch traced here: 70.2 us
  Pallas kernels  60.7 us (86%)
  local copies, waits for them, and re-layouts  8.82 us (13%)
    pallas_call x1, Pallas kernels, shards(): pl.pallas_call(kernel, out_shape=[jax.ShapeDtypeStruct((HALF, D), BF16),...  60.7 us
    unnamed x6, local copies, waits for them, and re-layouts  8.82 us

profile of v1, /device:TPU:1, one launch (start us, length us, event | category | flops | bytes accessed | tf_op | source)
XLA Modules:
  0.0 70.2 jit_solution(12473085919132539817)
XLA Ops:
  0.6 60.7 %shard_map.136 = (bf16[256,512]{1,0:T(8,128)(2,1)}, bf16[256,512]{1,0:T(8,128)(2,1)}, f32[8,384]{1,0:T(8,128)}, f32[8,128]{1,0:T(8,128)}, f32[1,512]{1,0:T(1,128)}, /*index=5*/f32[512,64]{1,0:T(8,128)}) custom-call(bf16[256,512]{1,0:T(8,128)(2,1)} %bitcast.10, bf16[256,512]{1,0:T(8,128)(2,1)} %teacher_ref.1, bf16[512,1536]{1,0:T(8,128)(2,1)} %wqkv_ref.1, ...), custom_call_target="tpu_custom_call" | custom-call | tf_op jit(solution)/shard_map/pallas_call | solution.py:367
  61.4 1.7 %copy.21 = bf16[1,256,512]{2,1,0:T(8,128)(2,1)} copy(bf16[1,256,512]{2,1,0:T(8,128)(2,1)} %bitcast.9) | data formatting | bytes 524288
  63.1 1.7 %copy.22 = bf16[1,256,512]{2,1,0:T(8,128)(2,1)} copy(bf16[1,256,512]{2,1,0:T(8,128)(2,1)} %bitcast.8) | data formatting | bytes 524288
  64.7 1.3 %copy.23 = f32[8,384]{1,0:T(8,128)} copy(f32[8,384]{1,0:T(8,128)} %get-tuple-element.26) | data formatting | bytes 24576
  66.0 1.3 %copy.24 = f32[8,128]{1,0:T(8,128)} copy(f32[8,128]{1,0:T(8,128)} %get-tuple-element.27) | data formatting | bytes 8192
  67.3 1.2 %copy.25 = f32[512]{0:T(512)} copy(f32[512]{0:T(512)} %bitcast.12) | data formatting | bytes 4096
  68.5 1.7 %copy.26 = f32[8,64,64]{2,1,0:T(8,128)} copy(f32[8,64,64]{2,1,0:T(8,128)} %bitcast.7) | data formatting | bytes 262144

commit v2 on v1

v2 whole, which is shorter than its diff:
```python
import functools

import jax
import jax.numpy as jnp
from jax import lax
from jax.experimental import pallas as pl
from jax.experimental.pallas import tpu as pltpu
from jax.sharding import PartitionSpec as P

D = 512
HEADS = 8
HD = 64
PIX = 64
ROWS = 4
SLOTS = 9
HALF = 256
EPS = 1e-06
NEG = -1e30
MESH = pl.DeviceIdType.MESH
F32 = jnp.float32
BF16 = jnp.bfloat16

NX, NY, NZ, NXL = 4, 4, 8, 2
N_TILE = NXL * NY * NZ

NN = (((1,), (0,)), ((), ()))
NT = (((1,), (1,)), ((), ()))
TN = (((0,), (0,)), ((), ()))


def mm(a, b, dims=NN):
    return lax.dot_general(a, b, dims, preferred_element_type=F32)


def kernel(
    x_hbm, teacher_hbm, wqkv_hbm, wout_hbm, gain_ref, bias_hbm, near_ref, valid_ref, orient_ref,
    out_hbm, dst_hbm, dwqkv_ref, dwout_ref, dgain_ref, dbias_ref,
    x_ref, teacher_ref, wqkv_ref, wout_ref, bias_ref, out_ref, dst_ref,
    xh, nb, nbt, kbuf, vbuf, tb, oh, qb, kg, vg, sref, pb, rinv, mixed, dmix, dout, dsb, dproj,
    qd, md, dcat, pcat, esend, erecv, turns,
    ga, ra, sa, ga1, ha1, ga2, ha2, ga3, ha3, ga4, ra4,
    gb, rb, sb, gb1, hb1, gb2, hb2, gb3, hb3, gb4, rb4,
    u0, ruz, w0, ruc, rux, ruy, fz, v0, vc, vx, vy, vz,
    send, recv, local,
):
    tile = lax.axis_index("tile")
    member = lax.axis_index("member")
    z = lax.rem(tile, NZ)
    y = lax.rem(tile // NZ, NY)
    x = (member // 2) * NXL + tile // (NZ * NY)
    core = lax.rem(member, 2)

    def at(x_=None, y_=None, z_=None, core_=None):
        x_ = x if x_ is None else x_
        y_ = y if y_ is None else y_
        z_ = z if z_ is None else z_
        core_ = core if core_ is None else core_
        return (lax.rem(x_, NXL) * NY + y_) * NZ + z_, (x_ // NXL) * 2 + core_

    right = (lax.rem(tile + 1, N_TILE), member)
    left = (lax.rem(tile + N_TILE - 1, N_TILE), member)
    sibling = at(core_=1 - core)
    xs = [lax.rem(x + o, NX) for o in range(1, NX)]
    ys = [lax.rem(y + o, NY) for o in range(1, NY)]
    zs = [lax.rem(z + o, NZ) for o in range(1, NZ)]
    peers = [left, right, sibling]
    peers += [at(x_=v) for v in xs] + [at(y_=v) for v in ys] + [at(z_=v) for v in zs]

    started = []
    moves = []

    def push(src, dst, to):
        n = len(started)
        copy = pltpu.make_async_remote_copy(
            src_ref=src, dst_ref=dst, send_sem=send.at[n], recv_sem=recv.at[n],
            device_id=to, device_id_type=MESH,
        )
        copy.start()
        started.append(copy)
        return copy

    def move(src, dst):
        copy = pltpu.make_async_copy(src, dst, local.at[len(moves)])
        copy.start()
        moves.append(copy)
        return copy

    def arrived(copies):
        for c in copies:
            c.wait_recv()

    barrier = pltpu.get_barrier_semaphore()
    for p in peers:
        pl.semaphore_signal(barrier, inc=1, device_id=p, device_id_type=MESH)
    load_x = move(x_hbm, x_ref)
    load_qkv = move(wqkv_hbm, wqkv_ref)
    load_bias = move(bias_hbm, bias_ref)
    load_out = move(wout_hbm, wout_ref)
    load_teacher = move(teacher_hbm, teacher_ref)
    pl.semaphore_wait(barrier, len(peers))

    states_moves = [push(x_hbm, xh.at[0], right), push(x_hbm, xh.at[1], left)]

    gain = gain_ref[...]

    def inverse_of(v32):
        return lax.rsqrt(jnp.mean(v32 * v32, axis=-1, keepdims=True) + EPS)

    def normalise(m, v):
        v32 = v.astype(F32)
        low = (v32 * inverse_of(v32) * gain).astype(BF16)
        nb[m * HALF:(m + 1) * HALF, :] = low
        nbt[:, m * HALF:(m + 1) * HALF] = low.T

    load_x.wait()
    normalise(1, x_ref[...])
    own = nb[HALF:2 * HALF, :]
    load_qkv.wait()
    qb[...] = (mm(own, wqkv_ref[:, :D]).astype(BF16) * 0.125).astype(BF16)

    def keys_values(m):
        rows = nb[m * HALF:(m + 1) * HALF, :]
        kbuf[m * ROWS:(m + 1) * ROWS] = mm(rows, wqkv_ref[:, D:2 * D]).astype(BF16).reshape(ROWS, PIX, D)
        vbuf[m * ROWS:(m + 1) * ROWS] = mm(rows, wqkv_ref[:, 2 * D:]).astype(BF16).reshape(ROWS, PIX, D)

    keys_values(1)

    load_bias.wait()
    j = lax.broadcasted_iota(jnp.int32, (PIX, 128), 0)
    l = lax.broadcasted_iota(jnp.int32, (PIX, 128), 1)
    u, w = j // 8, j % 8
    for o in range(4):
        oh[o] = jnp.where(l == u * 8 + w, 1.0, 0.0).astype(BF16)
        pick = jnp.where(l[:, :PIX] == (u * 8 + w)[:, :PIX], 1.0, 0.0)
        tb[o] = lax.dot_general(
            pick, bias_ref[...], NT, precision=lax.Precision.HIGHEST, preferred_element_type=F32
        )
        u, w = w, 7 - u
    tb[4] = jnp.full((PIX, D), NEG, F32)

    head_row = lax.broadcasted_iota(jnp.int32, (HALF, HALF), 0) // HD
    head_lane = lax.broadcasted_iota(jnp.int32, (HALF, HALF), 1) // HD
    same_head = jnp.where(head_row == head_lane, 1.0, 0.0).astype(BF16)
    lane_head = lax.broadcasted_iota(jnp.int32, (PIX, HALF), 1) // HD

    def block_diagonal(v):
        return jnp.concatenate([v] * 4, axis=0) * same_head

    def diagonal(v):
        out = v[:PIX]
        for a in range(1, 4):
            out = jnp.where(lane_head == a, v[a * PIX:(a + 1) * PIX], out)
        return out

    groups = [slice(0, HALF), slice(HALF, D)]
    tables = [[jnp.where(valid_ref[b, s] > 0, orient_ref[b, s], 4) for s in range(SLOTS)] for b in range(ROWS)]

    def score(b, slots):
        for s in slots:
            at_block = (s // 3) * ROWS + lax.rem(near_ref[b, s], ROWS)
            kg[b, s * PIX:(s + 1) * PIX, :] = kbuf[at_block]
            vg[b, s * PIX:(s + 1) * PIX, :] = vbuf[at_block]
        first, n = slots[0], len(slots)
        for g, lanes in enumerate(groups):
            scores = mm(kg[b, first * PIX:(first + n) * PIX, lanes], qd[g, b * HALF:(b + 1) * HALF, :], NT)
            for i, s in enumerate(slots):
                sref[b, s * PIX:(s + 1) * PIX, lanes] = scores[i * PIX:(i + 1) * PIX] + tb[tables[b][s], :, lanes]

    for b in range(ROWS):
        for g, lanes in enumerate(groups):
            qd[g, b * HALF:(b + 1) * HALF, :] = block_diagonal(qb[b * PIX:(b + 1) * PIX, lanes])
        score(b, (3, 4, 5))
        pb[b, SLOTS] = jnp.zeros((PIX, D), BF16)
        dsb[b, SLOTS] = jnp.zeros((PIX, D), BF16)
    dproj[:HALF, :D] = jnp.zeros((HALF, D), BF16)
    dproj[2 * HALF:, :D] = jnp.zeros((HALF, D), BF16)

    arrived(states_moves)
    normalise(0, xh[0])
    keys_values(0)
    normalise(2, xh[1])
    keys_values(2)

    for b in range(ROWS):
        score(b, (0, 1, 2))
        score(b, (6, 7, 8))
        for g, lanes in enumerate(groups):
            top = None
            for s in range(SLOTS):
                piece = sref[b, s * PIX:(s + 1) * PIX, lanes]
                top = piece if top is None else jnp.maximum(top, piece)
            top = jnp.max(top, axis=0, keepdims=True)
            total = None
            for s in range(SLOTS):
                piece = jnp.exp(sref[b, s * PIX:(s + 1) * PIX, lanes] - top)
                sref[b, s * PIX:(s + 1) * PIX, lanes] = piece
                total = piece if total is None else total + piece
            share = 1.0 / jnp.sum(total, axis=0, keepdims=True)
            rinv[b, :, lanes] = share
            for s in range(SLOTS):
                piece = sref[b, s * PIX:(s + 1) * PIX, lanes] * share
                pb[b, s, :, lanes] = piece.astype(BF16)
            probs = pb[b, 0:SLOTS, :, lanes].reshape(SLOTS * PIX, HALF)
            mixed[b * PIX:(b + 1) * PIX, lanes] = diagonal(mm(probs, vg[b, :, lanes], TN)).astype(BF16)

    load_out.wait()
    load_teacher.wait()
    out32 = x_ref[...].astype(F32) + mm(mixed[...], wout_ref[...])
    out_ref[...] = out32.astype(BF16)
    move(out_ref, out_hbm)
    dout[...] = (out32 - teacher_ref[...].astype(F32)).astype(BF16)
    dmix[...] = mm(dout[...], wout_ref[...], NT).astype(BF16)

    def lay_out(grads, c, xh_, value):
        low = value.astype(BF16)
        for xl in range(NXL):
            for yy in range(NY):
                for zh in range(2):
                    fb = (xl * NY + yy) * 2 + zh
                    grads[c, xh_, zh, xl, yy] = low[fb * 32:(fb + 1) * 32]

    def core_sum(grads, got, total):
        for xh_ in range(2):
            for zh in range(2):
                for xl in range(NXL):
                    total[zh, xh_ * NXL + xl] = (
                        grads[core, xh_, zh, xl].astype(F32) + got[xh_, zh, xl].astype(F32)
                    ).astype(BF16)

    def first_hops(total, by_x, by_y):
        copies = [push(total.at[0, v], by_x.at[o], at(x_=v)) for o, v in enumerate(xs)]
        return copies + [push(total.at[1, :, v], by_y.at[o], at(y_=v)) for o, v in enumerate(ys)]

    def first_sums(total, by_x, by_y, one, two):
        one[...] = (
            total[0, x].astype(F32) + by_x[0].astype(F32) + by_x[1].astype(F32) + by_x[2].astype(F32)
        ).astype(BF16)
        for xx in range(NX):
            two[xx] = (
                total[1, xx, y].astype(F32) + by_y[0, xx].astype(F32) + by_y[1, xx].astype(F32)
                + by_y[2, xx].astype(F32)
            ).astype(BF16)

    def second_hops(one, two, by_y, by_x):
        copies = [push(one.at[v], by_y.at[o], at(y_=v)) for o, v in enumerate(ys)]
        return copies + [push(two.at[v], by_x.at[o], at(x_=v)) for o, v in enumerate(xs)]

    def second_sums(one, two, by_y, by_x):
        ca = one[y].astype(F32) + by_y[0].astype(F32) + by_y[1].astype(F32) + by_y[2].astype(F32)
        cb = two[x].astype(F32) + by_x[0].astype(F32) + by_x[1].astype(F32) + by_x[2].astype(F32)
        return [(ca if i < 4 else cb)[(i % 4) * 8:(i % 4) * 8 + 8] for i in range(NZ)]

    grad_out = mm(mixed[...], dout[...], TN)
    for m in range(4):
        lay_out(ga, m % 2, m // 2, grad_out[:, m * 128:(m + 1) * 128])
    a_core = [push(ga.at[1 - core], ra, sibling)]

    dbias = None
    for b in range(ROWS):
        for g, lanes in enumerate(groups):
            diag = block_diagonal(dmix[b * PIX:(b + 1) * PIX, lanes])
            md[g, b * HALF:(b + 1) * HALF, :] = diag
            dprobs = mm(vg[b, :, lanes], diag, NT)
            share = rinv[b, :, lanes]
            total = None
            for s in range(SLOTS):
                piece = sref[b, s * PIX:(s + 1) * PIX, lanes] * dprobs[s * PIX:(s + 1) * PIX]
                total = piece if total is None else total + piece
            delta = jnp.sum(total, axis=0, keepdims=True) * share
            for s in range(SLOTS):
                piece = sref[b, s * PIX:(s + 1) * PIX, lanes] * share
                piece = piece * (dprobs[s * PIX:(s + 1) * PIX] - delta)
                dsb[b, s, :, lanes] = piece.astype(BF16)
            dscores = dsb[b, 0:SLOTS, :, lanes].reshape(SLOTS * PIX, HALF)
            dproj[HALF + b * PIX:HALF + (b + 1) * PIX, lanes] = (
                diagonal(mm(dscores, kg[b, :, lanes], TN)) * 0.125
            ).astype(BF16)
        for s in range(SLOTS):
            turns[s * PIX:(s + 1) * PIX, :] = oh[orient_ref[b, s]]
        term = mm(turns[...], dsb[b, 0:SLOTS].reshape(SLOTS * PIX, D), TN)[:PIX]
        dbias = term if dbias is None else dbias + term

    for i in range(NZ):
        u0[i] = jnp.concatenate(
            [dbias[i * 8:(i + 1) * 8, :HALF], dbias[i * 8:(i + 1) * 8, HALF:]], axis=0
        ).astype(BF16)
    u_z = [push(u0.at[v], ruz.at[o], at(z_=v)) for o, v in enumerate(zs)]

    arrived(a_core)
    core_sum(ga, ra, sa)
    a_first = first_hops(sa, ga1, ha1)

    for b in range(ROWS):
        rows = [lax.rem(near_ref[b, s], ROWS) for s in range(SLOTS)]
        for m in range(3):
            for t in range(ROWS):
                slots = [jnp.where(rows[3 * m + k] == t, 3 * m + k, SLOTS) for k in range(3)]
                here = slice((m * ROWS + t) * PIX, (m * ROWS + t + 1) * PIX)
                ds = dsb[b, slots[0]] + dsb[b, slots[1]] + dsb[b, slots[2]]
                ps = pb[b, slots[0]] + pb[b, slots[1]] + pb[b, slots[2]]
                for g, lanes in enumerate(groups):
                    dcat[g, here, b * HALF:(b + 1) * HALF] = ds[:, lanes]
                    pcat[g, here, b * HALF:(b + 1) * HALF] = ps[:, lanes]
    for g in range(2):
        dproj[:, D + g * HALF:D + (g + 1) * HALF] = mm(dcat[g], qd[g]).astype(BF16)
        dproj[:, 2 * D + g * HALF:2 * D + (g + 1) * HALF] = mm(pcat[g], md[g]).astype(BF16)

    def member_grads(c, xh_):
        lanes = pl.ds(pl.multiple_of((xh_ * 2 + c) * 384, 128), 384)
        lay_out(gb, c, xh_, mm(nbt[...], dproj[:, lanes]))

    b_core = []
    for xh_ in range(2):
        member_grads(1 - core, xh_)
        b_core.append(push(gb.at[1 - core, xh_], rb.at[xh_], sibling))

    wkv = wqkv_ref[:, D:]

    def scaled(v):
        v32 = v.astype(F32)
        return v32 * inverse_of(v32)

    def by_eight(v):
        return jnp.sum(v.reshape(HALF // 8, 8, D), axis=0)

    edge_l = mm(dproj[:HALF, D:], wkv, NT)
    esend[0] = edge_l.astype(BF16)
    e_moves = [push(esend.at[0], erecv.at[0], left)]
    edge_r = mm(dproj[2 * HALF:, D:], wkv, NT)
    esend[1] = edge_r.astype(BF16)
    e_moves.append(push(esend.at[1], erecv.at[1], right))

    for xh_ in range(2):
        member_grads(core, xh_)

    arrived(a_first)
    first_sums(sa, ga1, ha1, ga2, ha2)
    a_second = second_hops(ga2, ha2, ga3, ha3)

    arrived(b_core)
    core_sum(gb, rb, sb)
    b_first = first_hops(sb, gb1, hb1)

    arrived(u_z)
    total = u0[z].astype(F32)
    for o in range(NZ - 1):
        total = total + ruz[o].astype(F32)
    w0[...] = total
    u_core = [push(w0, ruc, sibling)]

    gain8 = by_eight(edge_l * scaled(xh[0])) + by_eight(edge_r * scaled(xh[1]))
    dnorm = mm(dproj[HALF:2 * HALF, :], wqkv_ref[...], NT)
    gain8 = gain8 + by_eight(dnorm * scaled(x_ref[...]))
    gain1 = jnp.sum(gain8, axis=0, keepdims=True)
    v0[...] = jnp.concatenate([gain1[:, i * 128:(i + 1) * 128] for i in range(4)] * 2, axis=0)
    v_core = [push(v0, vc, sibling)]

    arrived(u_core)
    rux[x] = w0[...] + ruc[...]
    u_x = [push(rux.at[x], rux.at[x], at(x_=v)) for v in xs]
    arrived(v_core)
    vx[x] = v0[...] + vc[...]
    v_x = [push(vx.at[x], vx.at[x], at(x_=v)) for v in xs]

    arrived(a_second)
    for i, value in enumerate(second_sums(ga2, ha2, ga3, ha3)):
        ga4[i] = value
    a_third = [push(ga4.at[v], ra4.at[o], at(z_=v)) for o, v in enumerate(zs)]

    arrived(b_first)
    first_sums(sb, gb1, hb1, gb2, hb2)
    b_second = second_hops(gb2, hb2, gb3, hb3)
    arrived(u_x)
    ruy[y] = rux[0] + rux[1] + rux[2] + rux[3]
    u_y = [push(ruy.at[y], ruy.at[y], at(y_=v)) for v in ys]
    arrived(v_x)
    vy[y] = vx[0] + vx[1] + vx[2] + vx[3]
    v_y = [push(vy.at[y], vy.at[y], at(y_=v)) for v in ys]

    arrived(e_moves)
    dnorm = dnorm + erecv[0].astype(F32) + erecv[1].astype(F32)
    x32 = x_ref[...].astype(F32)
    inverse = inverse_of(x32)
    dscaled = dnorm * gain
    dst_ref[...] = (
        dout[...].astype(F32)
        + inverse * dscaled
        - x32 * (inverse * inverse * inverse * jnp.mean(dscaled * x32, axis=-1, keepdims=True))
    ).astype(BF16)
    move(dst_ref, dst_hbm)

    arrived(b_second)
    for i, value in enumerate(second_sums(gb2, hb2, gb3, hb3)):
        gb4[i] = jnp.concatenate(
            [value[:, :HALF], jnp.concatenate([value[:, HALF:], value[:, HALF:]], axis=1)], axis=0
        ).astype(BF16)
    b_third = [push(gb4.at[v], rb4.at[o], at(z_=v)) for o, v in enumerate(zs)]
    arrived(u_y)
    fz[z] = (ruy[0] + ruy[1] + ruy[2] + ruy[3]).astype(BF16)
    f_z = [push(fz.at[z], fz.at[z], at(z_=v)) for v in zs]
    arrived(v_y)
    vz[z] = vy[0] + vy[1] + vy[2] + vy[3]
    v_z = [push(vz.at[z], vz.at[z], at(z_=v)) for v in zs]

    arrived(a_third)
    final = ga4[z]
    for o in range(NZ - 1):
        final = final + ra4[o]
    dwout_ref[...] = final
    arrived(b_third)
    final = gb4[z].astype(F32)
    for o in range(NZ - 1):
        final = final + rb4[o].astype(F32)
    dwqkv_ref[:, :HALF] = final[:8]
    dwqkv_ref[:, HALF:] = final[8:, :128]
    arrived(f_z)
    for i in range(NZ):
        value = fz[i].astype(F32)
        dbias_ref[i * 8:(i + 1) * 8, :HALF] = value[:8]
        dbias_ref[i * 8:(i + 1) * 8, HALF:] = value[8:]
    arrived(v_z)
    total = vz[0]
    for i in range(1, NZ):
        total = total + vz[i]
    for i in range(4):
        dgain_ref[:, i * 128:(i + 1) * 128] = total[i:i + 1]

    for c in started:
        c.wait_send()
    moves[-2].wait()
    moves[-1].wait()


def deliver(*refs):
    for i in range(5):
        refs[6 + i][...] = refs[i][...]
    refs[11][...] = refs[5][...].T


N_CHAIN = 6 + 6 + 7
N_COPIES = 2 + 2 + (1 + N_CHAIN) + (2 + N_CHAIN) + (7 + 1 + 3 + 3 + 7) + (1 + 3 + 3 + 7)


def scratch():
    def v(*shape, kind=BF16):
        return pltpu.VMEM(shape, kind)

    def chain(columns, last, kind):
        return [
            v(2, 2, 2, NXL, NY, 32, columns), v(2, 2, NXL, NY, 32, columns), v(2, NX, NY, 32, columns),
            v(NX - 1, NY, 32, columns), v(NY - 1, NX, 32, columns), v(NY, 32, columns), v(NX, 32, columns),
            v(NY - 1, 32, columns), v(NX - 1, 32, columns), v(NZ, *last, kind=kind), v(NZ - 1, *last, kind=kind),
        ]

    return [
        v(HALF, D), v(HALF, D), v(D, 3 * D), v(D, D), v(HEADS * PIX, PIX, kind=F32), v(HALF, D), v(HALF, D),
        v(2, HALF, D), v(3 * HALF, D), v(D, 3 * HALF), v(12, PIX, D), v(12, PIX, D), v(5, PIX, D, kind=F32),
        v(4, PIX, 128),
        v(HALF, D), v(ROWS, SLOTS * PIX, D), v(ROWS, SLOTS * PIX, D), v(ROWS, SLOTS * PIX, D, kind=F32),
        v(ROWS, SLOTS + 1, PIX, D), v(ROWS, 1, D, kind=F32), v(HALF, D), v(HALF, D), v(HALF, D),
        v(ROWS, SLOTS + 1, PIX, D), v(3 * HALF, 3 * D),
        v(2, ROWS * HALF, HALF), v(2, ROWS * HALF, HALF), v(2, 12 * PIX, ROWS * HALF), v(2, 12 * PIX, ROWS * HALF),
        v(2, HALF, D), v(2, HALF, D), v(SLOTS * PIX, 128),
        *chain(128, (8, 128), F32),
        *chain(384, (16, HALF), BF16),
        v(NZ, 16, HALF), v(NZ - 1, 16, HALF), v(16, HALF, kind=F32), v(16, HALF, kind=F32),
        v(NX, 16, HALF, kind=F32), v(NY, 16, HALF, kind=F32), v(NZ, 16, HALF),
        v(8, 128, kind=F32), v(8, 128, kind=F32), v(NX, 8, 128, kind=F32), v(NY, 8, 128, kind=F32),
        v(NZ, 8, 128, kind=F32),
        pltpu.SemaphoreType.DMA((N_COPIES,)), pltpu.SemaphoreType.DMA((N_COPIES,)), pltpu.SemaphoreType.DMA((7,)),
    ]


def shards(states, teacher, w_qkv, w_out, gain, bias, neighbours, valid, orient):
    vmem = pl.BlockSpec(memory_space=pltpu.VMEM)
    anywhere = pl.BlockSpec(memory_space=pl.ANY)
    smem = pl.BlockSpec(memory_space=pltpu.SMEM)
    shapes = [
        jax.ShapeDtypeStruct((HALF, D), BF16),
        jax.ShapeDtypeStruct((HALF, D), BF16),
        jax.ShapeDtypeStruct((8, 384), F32),
        jax.ShapeDtypeStruct((8, 128), F32),
        jax.ShapeDtypeStruct((1, D), F32),
        jax.ShapeDtypeStruct((PIX, D), F32),
    ]
    results = pl.pallas_call(
        kernel,
        out_shape=shapes,
        in_specs=[anywhere] * 4 + [vmem, anywhere] + [smem] * 3,
        out_specs=[anywhere] * 2 + [vmem] * 4,
        scratch_shapes=scratch(),
        compiler_params=pltpu.CompilerParams(
            collective_id=0, has_side_effects=True, vmem_limit_bytes=60 * 2**20
        ),
    )(
        states[0], teacher, w_qkv, w_out, gain.reshape(1, D), bias.reshape(HEADS * PIX, PIX),
        neighbours, valid, orient,
    )
    output, d_states, d_wqkv, d_wout, d_gain, d_bias = pl.pallas_call(
        deliver,
        out_shape=shapes[:5] + [jax.ShapeDtypeStruct((HEADS * PIX, PIX), F32)],
        in_specs=[vmem] * 6,
        out_specs=[vmem] * 6,
    )(*results)
    return output[None], d_states[None], d_wqkv, d_wout, d_gain[0], d_bias.reshape(HEADS, PIX, PIX)


def solution(mesh):
    return jax.shard_map(
        shards,
        mesh=mesh,
        in_specs=(
            P("member", "tile", None), P("tile", None), P(), P(), P(), P(),
            P("tile", None), P("tile", None), P("tile", None),
        ),
        out_specs=(
            P("member", "tile", None), P("member", "tile", None), P("tile", "member"), P("tile", "member"), P(), P(),
        ),
        check_vma=False,
    )
```

time: 70.5 us -> 56.8 us (0.81)
  local copies, waits for them, and re-layouts: 8.82 us -> 0 us
  Pallas kernels: 60.7 us -> 55.5 us
    unnamed x6 -> x0, local copies, waits for them, and re-layouts: 8.82 us -> none
    pallas_call x1 -> x2, Pallas kernels: 60.7 us -> 55.5 us  [the longest x1 53.4 us: shards(): pl.pallas_call(kernel, out_shape=shapes, in_specs=[anywhere] * 4 + [vmem,...]
where the time goes in v2:
time: 56.8 us; the launch traced here: 56.1 us
  Pallas kernels  55.5 us (98%)
  between operations  0.64 us (1%)
    pallas_call x1, Pallas kernels, shards(): pl.pallas_call(kernel, out_shape=shapes, in_specs=[anywhere] * 4 + [vmem,...  53.4 us
    pallas_call x1, Pallas kernels, shards(): pl.pallas_call(deliver, out_shape=shapes[:5] + [jax.ShapeDtypeStruct((HEA...  2.03 us

profile of v2, /device:TPU:1, one launch (start us, length us, event | category | flops | bytes accessed | tf_op | source)
XLA Modules:
  0.0 56.1 jit_solution(5313323080016148427)
XLA Ops:
  0.6 53.4 %shard_map.136 = (bf16[256,512]{1,0:T(8,128)(2,1)}, bf16[256,512]{1,0:T(8,128)(2,1)}, f32[8,384]{1,0:T(8,128)}, f32[8,128]{1,0:T(8,128)}, f32[1,512]{1,0:T(1,128)}, /*index=5*/f32[64,512]{1,0:T(8,128)}) custom-call(bf16[256,512]{1,0:T(8,128)(2,1)} %bitcast.7, bf16[256,512]{1,0:T(8,128)(2,1)} %teacher_hbm.1, bf16[512,1536]{1,0:T(8,128)(2,1)} %wqkv_hbm.1, ...), custom_call_target="tpu_custom_call" | custom-call | tf_op jit(solution)/shard_map/pallas_call | solution.py:486
  54.1 2.0 %shard_map.137 = (bf16[256,512]{1,0:T(8,128)(2,1)}, bf16[256,512]{1,0:T(8,128)(2,1)}, f32[8,384]{1,0:T(8,128)}, f32[8,128]{1,0:T(8,128)}, f32[1,512]{1,0:T(1,128)}, /*index=5*/f32[512,64]{1,0:T(8,128)}) custom-call(bf16[256,512]{1,0:T(8,128)(2,1)} %get-tuple-element.18.refs_0_, bf16[256,512]{1,0:T(8,128)(2,1)} %get-tuple-element.19.refs_1_, ...), custom_call_target="tpu_custom_call" | custom-call | tf_op jit(solution)/shard_map/pallas_call | solution.py:499

commit v3 on v2

--- a/solution.py
+++ b/solution.py
@@ -22,6 +22,7 @@
 
 NX, NY, NZ, NXL = 4, 4, 8, 2
 N_TILE = NXL * NY * NZ
+SPLIT = 32
 
 NN = (((1,), (0,)), ((), ()))
 NT = (((1,), (1,)), ((), ()))
@@ -33,13 +34,12 @@
 
 
 def kernel(
-    x_hbm, teacher_hbm, wqkv_hbm, wout_hbm, gain_ref, bias_hbm, near_ref, valid_ref, orient_ref,
+    x_hbm, teacher_hbm, wqkv_hbm, wout_hbm, gain_hbm, bias_hbm, near_hbm, valid_hbm, orient_hbm,
     out_hbm, dst_hbm, dwqkv_ref, dwout_ref, dgain_ref, dbias_ref,
-    x_ref, teacher_ref, wqkv_ref, wout_ref, bias_ref, out_ref, dst_ref,
-    xh, nb, nbt, kbuf, vbuf, tb, oh, qb, kg, vg, sref, pb, rinv, mixed, dmix, dout, dsb, dproj,
+    x_ref, teacher_ref, wqkv_ref, wout_ref, gain_ref, bias_ref, near_ref, valid_ref, orient_ref, out_ref, dst_ref,
+    xh, nb, nbt, kbuf, vbuf, tb, oh, qb, kg, vg, sref, peak, pb, rinv, mixed, dmix, dout, dsb, dproj,
     qd, md, dcat, pcat, esend, erecv, turns,
-    ga, ra, sa, ga1, ha1, ga2, ha2, ga3, ha3, ga4, ra4,
-    gb, rb, sb, gb1, hb1, gb2, hb2, gb3, hb3, gb4, rb4,
+    ga, ra, sa, ya, ga1, ha1, gb, rb, sb, yb, gb1, hb1, g2, h2, g3, h3, g4, r4,
     u0, ruz, w0, ruc, rux, ruy, fz, v0, vc, vx, vy, vz,
     send, recv, local,
 ):
@@ -85,6 +85,13 @@
         moves.append(copy)
         return copy
 
+    left_over = []
+
+    def all_sent():
+        for c in started[len(left_over):]:
+            c.wait_send()
+            left_over.append(c)
+
     def arrived(copies):
         for c in copies:
             c.wait_recv()
@@ -92,15 +99,19 @@
     barrier = pltpu.get_barrier_semaphore()
     for p in peers:
         pl.semaphore_signal(barrier, inc=1, device_id=p, device_id_type=MESH)
+    pl.semaphore_wait(barrier, len(peers))
+
+    states_moves = [push(x_hbm, xh.at[0], right), push(x_hbm, xh.at[1], left)]
+
     load_x = move(x_hbm, x_ref)
+    load_gain = move(gain_hbm, gain_ref)
     load_qkv = move(wqkv_hbm, wqkv_ref)
     load_bias = move(bias_hbm, bias_ref)
+    load_tables = [move(near_hbm, near_ref), move(valid_hbm, valid_ref), move(orient_hbm, orient_ref)]
     load_out = move(wout_hbm, wout_ref)
     load_teacher = move(teacher_hbm, teacher_ref)
-    pl.semaphore_wait(barrier, len(peers))
-
-    states_moves = [push(x_hbm, xh.at[0], right), push(x_hbm, xh.at[1], left)]
-
+
+    load_gain.wait()
     gain = gain_ref[...]
 
     def inverse_of(v32):
@@ -153,9 +164,11 @@
         return out
 
     groups = [slice(0, HALF), slice(HALF, D)]
+    for c in load_tables:
+        c.wait()
     tables = [[jnp.where(valid_ref[b, s] > 0, orient_ref[b, s], 4) for s in range(SLOTS)] for b in range(ROWS)]
 
-    def score(b, slots):
+    def score(b, slots, tops):
         for s in slots:
             at_block = (s // 3) * ROWS + lax.rem(near_ref[b, s], ROWS)
             kg[b, s * PIX:(s + 1) * PIX, :] = kbuf[at_block]
@@ -164,12 +177,17 @@
         for g, lanes in enumerate(groups):
             scores = mm(kg[b, first * PIX:(first + n) * PIX, lanes], qd[g, b * HALF:(b + 1) * HALF, :], NT)
             for i, s in enumerate(slots):
-                sref[b, s * PIX:(s + 1) * PIX, lanes] = scores[i * PIX:(i + 1) * PIX] + tb[tables[b][s], :, lanes]
+                piece = scores[i * PIX:(i + 1) * PIX] + tb[tables[b][s], :, lanes]
+                sref[b, s * PIX:(s + 1) * PIX, lanes] = piece
+                tops[g] = piece if tops[g] is None else jnp.maximum(tops[g], piece)
 
     for b in range(ROWS):
         for g, lanes in enumerate(groups):
             qd[g, b * HALF:(b + 1) * HALF, :] = block_diagonal(qb[b * PIX:(b + 1) * PIX, lanes])
-        score(b, (3, 4, 5))
+        tops = [None, None]
+        score(b, (3, 4, 5), tops)
+        for g, lanes in enumerate(groups):
+            peak[b, :, lanes] = tops[g]
         pb[b, SLOTS] = jnp.zeros((PIX, D), BF16)
         dsb[b, SLOTS] = jnp.zeros((PIX, D), BF16)
     dproj[:HALF, :D] = jnp.zeros((HALF, D), BF16)
@@ -182,14 +200,11 @@
     keys_values(2)
 
     for b in range(ROWS):
-        score(b, (0, 1, 2))
-        score(b, (6, 7, 8))
+        tops = [peak[b, :, lanes] for lanes in groups]
+        score(b, (0, 1, 2), tops)
+        score(b, (6, 7, 8), tops)
         for g, lanes in enumerate(groups):
-            top = None
-            for s in range(SLOTS):
-                piece = sref[b, s * PIX:(s + 1) * PIX, lanes]
-                top = piece if top is None else jnp.maximum(top, piece)
-            top = jnp.max(top, axis=0, keepdims=True)
+            top = jnp.max(tops[g], axis=0, keepdims=True)
             total = None
             for s in range(SLOTS):
                 piece = jnp.exp(sref[b, s * PIX:(s + 1) * PIX, lanes] - top)
@@ -215,40 +230,29 @@
         low = value.astype(BF16)
         for xl in range(NXL):
             for yy in range(NY):
-                for zh in range(2):
-                    fb = (xl * NY + yy) * 2 + zh
-                    grads[c, xh_, zh, xl, yy] = low[fb * 32:(fb + 1) * 32]
-
-    def core_sum(grads, got, total):
+                fb = xl * NY + yy
+                grads[c, xh_, xl, yy] = low[fb * 64:(fb + 1) * 64]
+
+    def core_sum(grads, got, one, two):
         for xh_ in range(2):
-            for zh in range(2):
-                for xl in range(NXL):
-                    total[zh, xh_ * NXL + xl] = (
-                        grads[core, xh_, zh, xl].astype(F32) + got[xh_, zh, xl].astype(F32)
-                    ).astype(BF16)
-
-    def first_hops(total, by_x, by_y):
-        copies = [push(total.at[0, v], by_x.at[o], at(x_=v)) for o, v in enumerate(xs)]
-        return copies + [push(total.at[1, :, v], by_y.at[o], at(y_=v)) for o, v in enumerate(ys)]
-
-    def first_sums(total, by_x, by_y, one, two):
-        one[...] = (
-            total[0, x].astype(F32) + by_x[0].astype(F32) + by_x[1].astype(F32) + by_x[2].astype(F32)
+            for xl in range(NXL):
+                total = (grads[core, xh_, xl].astype(F32) + got[xh_, xl].astype(F32)).astype(BF16)
+                one[xh_ * NXL + xl] = total[:, :SPLIT]
+                two[xh_ * NXL + xl] = total[:, SPLIT:]
+
+    def first_hops(one, two, by_x, by_y):
+        copies = [push(two.at[:, v], by_y.at[o], at(y_=v)) for o, v in enumerate(ys)]
+        return copies + [push(one.at[v], by_x.at[o], at(x_=v)) for o, v in enumerate(xs)]
+
+    def first_sums(one, two, by_x, by_y, lanes):
+        g2[:, :, lanes] = (
+            one[x].astype(F32) + by_x[0].astype(F32) + by_x[1].astype(F32) + by_x[2].astype(F32)
         ).astype(BF16)
         for xx in range(NX):
-            two[xx] = (
-                total[1, xx, y].astype(F32) + by_y[0, xx].astype(F32) + by_y[1, xx].astype(F32)
+            h2[xx, :, lanes] = (
+                two[xx, y].astype(F32) + by_y[0, xx].astype(F32) + by_y[1, xx].astype(F32)
                 + by_y[2, xx].astype(F32)
             ).astype(BF16)
-
-    def second_hops(one, two, by_y, by_x):
-        copies = [push(one.at[v], by_y.at[o], at(y_=v)) for o, v in enumerate(ys)]
-        return copies + [push(two.at[v], by_x.at[o], at(x_=v)) for o, v in enumerate(xs)]
-
-    def second_sums(one, two, by_y, by_x):
-        ca = one[y].astype(F32) + by_y[0].astype(F32) + by_y[1].astype(F32) + by_y[2].astype(F32)
-        cb = two[x].astype(F32) + by_x[0].astype(F32) + by_x[1].astype(F32) + by_x[2].astype(F32)
-        return [(ca if i < 4 else cb)[(i % 4) * 8:(i % 4) * 8 + 8] for i in range(NZ)]
 
     grad_out = mm(mixed[...], dout[...], TN)
     for m in range(4):
@@ -287,8 +291,8 @@
     u_z = [push(u0.at[v], ruz.at[o], at(z_=v)) for o, v in enumerate(zs)]
 
     arrived(a_core)
-    core_sum(ga, ra, sa)
-    a_first = first_hops(sa, ga1, ha1)
+    core_sum(ga, ra, sa, ya)
+    a_first = first_hops(sa, ya, ga1, ha1)
 
     for b in range(ROWS):
         rows = [lax.rem(near_ref[b, s], ROWS) for s in range(SLOTS)]
@@ -305,15 +309,6 @@
         dproj[:, D + g * HALF:D + (g + 1) * HALF] = mm(dcat[g], qd[g]).astype(BF16)
         dproj[:, 2 * D + g * HALF:2 * D + (g + 1) * HALF] = mm(pcat[g], md[g]).astype(BF16)
 
-    def member_grads(c, xh_):
-        lanes = pl.ds(pl.multiple_of((xh_ * 2 + c) * 384, 128), 384)
-        lay_out(gb, c, xh_, mm(nbt[...], dproj[:, lanes]))
-
-    b_core = []
-    for xh_ in range(2):
-        member_grads(1 - core, xh_)
-        b_core.append(push(gb.at[1 - core, xh_], rb.at[xh_], sibling))
-
     wkv = wqkv_ref[:, D:]
 
     def scaled(v):
@@ -330,16 +325,14 @@
     esend[1] = edge_r.astype(BF16)
     e_moves.append(push(esend.at[1], erecv.at[1], right))
 
+    def member_grads(c, xh_):
+        lanes = pl.ds(pl.multiple_of((xh_ * 2 + c) * 384, 128), 384)
+        lay_out(gb, c, xh_, mm(nbt[...], dproj[:, lanes]))
+
+    b_core = []
     for xh_ in range(2):
-        member_grads(core, xh_)
-
-    arrived(a_first)
-    first_sums(sa, ga1, ha1, ga2, ha2)
-    a_second = second_hops(ga2, ha2, ga3, ha3)
-
-    arrived(b_core)
-    core_sum(gb, rb, sb)
-    b_first = first_hops(sb, gb1, hb1)
+        member_grads(1 - core, xh_)
+        b_core.append(push(gb.at[1 - core, xh_], rb.at[xh_], sibling))
 
     arrived(u_z)
     total = u0[z].astype(F32)
@@ -348,6 +341,20 @@
     w0[...] = total
     u_core = [push(w0, ruc, sibling)]
 
+    for xh_ in range(2):
+        member_grads(core, xh_)
+
+    arrived(a_first)
+    first_sums(sa, ya, ga1, ha1, slice(384, D))
+
+    arrived(u_core)
+    rux[x] = w0[...] + ruc[...]
+    u_x = [push(rux.at[x], rux.at[x], at(x_=v)) for v in xs]
+
+    arrived(b_core)
+    core_sum(gb, rb, sb, yb)
+    b_first = first_hops(sb, yb, gb1, hb1)
+
     gain8 = by_eight(edge_l * scaled(xh[0])) + by_eight(edge_r * scaled(xh[1]))
     dnorm = mm(dproj[HALF:2 * HALF, :], wqkv_ref[...], NT)
     gain8 = gain8 + by_eight(dnorm * scaled(x_ref[...]))
@@ -355,27 +362,28 @@
     v0[...] = jnp.concatenate([gain1[:, i * 128:(i + 1) * 128] for i in range(4)] * 2, axis=0)
     v_core = [push(v0, vc, sibling)]
 
-    arrived(u_core)
-    rux[x] = w0[...] + ruc[...]
-    u_x = [push(rux.at[x], rux.at[x], at(x_=v)) for v in xs]
+    arrived(u_x)
+    ruy[y] = rux[0] + rux[1] + rux[2] + rux[3]
+    u_y = [push(ruy.at[y], ruy.at[y], at(y_=v)) for v in ys]
     arrived(v_core)
     vx[x] = v0[...] + vc[...]
     v_x = [push(vx.at[x], vx.at[x], at(x_=v)) for v in xs]
 
-    arrived(a_second)
-    for i, value in enumerate(second_sums(ga2, ha2, ga3, ha3)):
-        ga4[i] = value
-    a_third = [push(ga4.at[v], ra4.at[o], at(z_=v)) for o, v in enumerate(zs)]
-
     arrived(b_first)
-    first_sums(sb, gb1, hb1, gb2, hb2)
-    b_second = second_hops(gb2, hb2, gb3, hb3)
-    arrived(u_x)
-    ruy[y] = rux[0] + rux[1] + rux[2] + rux[3]
-    u_y = [push(ruy.at[y], ruy.at[y], at(y_=v)) for v in ys]
+    first_sums(sb, yb, gb1, hb1, slice(0, 384))
+    second = [push(g2.at[v], g3.at[o], at(y_=v)) for o, v in enumerate(ys)]
+    second += [push(h2.at[v], h3.at[o], at(x_=v)) for o, v in enumerate(xs)]
+    arrived(u_y)
+    fz[z] = (ruy[0] + ruy[1] + ruy[2] + ruy[3]).astype(BF16)
+    f_z = [push(fz.at[z], fz.at[z], at(z_=v)) for v in zs]
     arrived(v_x)
     vy[y] = vx[0] + vx[1] + vx[2] + vx[3]
     v_y = [push(vy.at[y], vy.at[y], at(y_=v)) for v in ys]
+
+    before = len(started) - len(second) - len(f_z) - len(v_y)
+    for c in started[:before]:
+        c.wait_send()
+        left_over.append(c)
 
     arrived(e_moves)
     dnorm = dnorm + erecv[0].astype(F32) + erecv[1].astype(F32)
@@ -389,30 +397,24 @@
     ).astype(BF16)
     move(dst_ref, dst_hbm)
 
-    arrived(b_second)
-    for i, value in enumerate(second_sums(gb2, hb2, gb3, hb3)):
-        gb4[i] = jnp.concatenate(
-            [value[:, :HALF], jnp.concatenate([value[:, HALF:], value[:, HALF:]], axis=1)], axis=0
-        ).astype(BF16)
-    b_third = [push(gb4.at[v], rb4.at[o], at(z_=v)) for o, v in enumerate(zs)]
-    arrived(u_y)
-    fz[z] = (ruy[0] + ruy[1] + ruy[2] + ruy[3]).astype(BF16)
-    f_z = [push(fz.at[z], fz.at[z], at(z_=v)) for v in zs]
+    arrived(second)
+    ca = g2[y].astype(F32) + g3[0].astype(F32) + g3[1].astype(F32) + g3[2].astype(F32)
+    cb = h2[x].astype(F32) + h3[0].astype(F32) + h3[1].astype(F32) + h3[2].astype(F32)
+    for i in range(NZ):
+        value = (ca if i < 4 else cb)[(i % 4) * 8:(i % 4) * 8 + 8]
+        g4[i] = jnp.concatenate([value[:, :HALF], value[:, HALF:]], axis=0).astype(BF16)
+    third = [push(g4.at[v], r4.at[o], at(z_=v)) for o, v in enumerate(zs)]
     arrived(v_y)
     vz[z] = vy[0] + vy[1] + vy[2] + vy[3]
     v_z = [push(vz.at[z], vz.at[z], at(z_=v)) for v in zs]
 
-    arrived(a_third)
-    final = ga4[z]
+    arrived(third)
+    final = g4[z].astype(F32)
     for o in range(NZ - 1):
-        final = final + ra4[o]
-    dwout_ref[...] = final
-    arrived(b_third)
-    final = gb4[z].astype(F32)
-    for o in range(NZ - 1):
-        final = final + rb4[o].astype(F32)
+        final = final + r4[o].astype(F32)
     dwqkv_ref[:, :HALF] = final[:8]
     dwqkv_ref[:, HALF:] = final[8:, :128]
+    dwout_ref[...] = final[8:, 128:]
     arrived(f_z)
     for i in range(NZ):
         value = fz[i].astype(F32)
@@ -425,8 +427,7 @@
     for i in range(4):
         dgain_ref[:, i * 128:(i + 1) * 128] = total[i:i + 1]
 
-    for c in started:
-        c.wait_send()
+    all_sent()
     moves[-2].wait()
     moves[-1].wait()
 
@@ -437,44 +438,45 @@
     refs[11][...] = refs[5][...].T
 
 
-N_CHAIN = 6 + 6 + 7
-N_COPIES = 2 + 2 + (1 + N_CHAIN) + (2 + N_CHAIN) + (7 + 1 + 3 + 3 + 7) + (1 + 3 + 3 + 7)
+N_COPIES = 2 + 2 + (1 + 6) + (2 + 6) + 6 + 7 + (7 + 1 + 3 + 3 + 7) + (1 + 3 + 3 + 7)
 
 
 def scratch():
     def v(*shape, kind=BF16):
         return pltpu.VMEM(shape, kind)
 
-    def chain(columns, last, kind):
+    def chain(columns):
         return [
-            v(2, 2, 2, NXL, NY, 32, columns), v(2, 2, NXL, NY, 32, columns), v(2, NX, NY, 32, columns),
-            v(NX - 1, NY, 32, columns), v(NY - 1, NX, 32, columns), v(NY, 32, columns), v(NX, 32, columns),
-            v(NY - 1, 32, columns), v(NX - 1, 32, columns), v(NZ, *last, kind=kind), v(NZ - 1, *last, kind=kind),
+            v(2, 2, NXL, NY, 64, columns), v(2, NXL, NY, 64, columns),
+            v(NX, NY, SPLIT, columns), v(NX, NY, 64 - SPLIT, columns),
+            v(NX - 1, NY, SPLIT, columns), v(NY - 1, NX, 64 - SPLIT, columns),
         ]
 
     return [
-        v(HALF, D), v(HALF, D), v(D, 3 * D), v(D, D), v(HEADS * PIX, PIX, kind=F32), v(HALF, D), v(HALF, D),
+        v(HALF, D), v(HALF, D), v(D, 3 * D), v(D, D), v(1, D, kind=F32), v(HEADS * PIX, PIX, kind=F32),
+        *[pltpu.SMEM((ROWS, SLOTS), jnp.int32)] * 3, v(HALF, D), v(HALF, D),
         v(2, HALF, D), v(3 * HALF, D), v(D, 3 * HALF), v(12, PIX, D), v(12, PIX, D), v(5, PIX, D, kind=F32),
         v(4, PIX, 128),
         v(HALF, D), v(ROWS, SLOTS * PIX, D), v(ROWS, SLOTS * PIX, D), v(ROWS, SLOTS * PIX, D, kind=F32),
+        v(ROWS, PIX, D, kind=F32),
         v(ROWS, SLOTS + 1, PIX, D), v(ROWS, 1, D, kind=F32), v(HALF, D), v(HALF, D), v(HALF, D),
         v(ROWS, SLOTS + 1, PIX, D), v(3 * HALF, 3 * D),
         v(2, ROWS * HALF, HALF), v(2, ROWS * HALF, HALF), v(2, 12 * PIX, ROWS * HALF), v(2, 12 * PIX, ROWS * HALF),
         v(2, HALF, D), v(2, HALF, D), v(SLOTS * PIX, 128),
-        *chain(128, (8, 128), F32),
-        *chain(384, (16, HALF), BF16),
+        *chain(128), *chain(384),
+        v(NY, SPLIT, D), v(NX, 64 - SPLIT, D), v(NY - 1, SPLIT, D), v(NX - 1, 64 - SPLIT, D),
+        v(NZ, 16, HALF), v(NZ - 1, 16, HALF),
         v(NZ, 16, HALF), v(NZ - 1, 16, HALF), v(16, HALF, kind=F32), v(16, HALF, kind=F32),
         v(NX, 16, HALF, kind=F32), v(NY, 16, HALF, kind=F32), v(NZ, 16, HALF),
         v(8, 128, kind=F32), v(8, 128, kind=F32), v(NX, 8, 128, kind=F32), v(NY, 8, 128, kind=F32),
         v(NZ, 8, 128, kind=F32),
-        pltpu.SemaphoreType.DMA((N_COPIES,)), pltpu.SemaphoreType.DMA((N_COPIES,)), pltpu.SemaphoreType.DMA((7,)),
+        pltpu.SemaphoreType.DMA((N_COPIES,)), pltpu.SemaphoreType.DMA((N_COPIES,)), pltpu.SemaphoreType.DMA((11,)),
     ]
 
 
 def shards(states, teacher, w_qkv, w_out, gain, bias, neighbours, valid, orient):
     vmem = pl.BlockSpec(memory_space=pltpu.VMEM)
     anywhere = pl.BlockSpec(memory_space=pl.ANY)
-    smem = pl.BlockSpec(memory_space=pltpu.SMEM)
     shapes = [
         jax.ShapeDtypeStruct((HALF, D), BF16),
         jax.ShapeDtypeStruct((HALF, D), BF16),
@@ -486,7 +488,7 @@
     results = pl.pallas_call(
         kernel,
         out_shape=shapes,
-        in_specs=[anywhere] * 4 + [vmem, anywhere] + [smem] * 3,
+        in_specs=[anywhere] * 9,
         out_specs=[anywhere] * 2 + [vmem] * 4,
         scratch_shapes=scratch(),
         compiler_params=pltpu.CompilerParams(

time: 56.8 us -> 55.9 us (0.984)
  Pallas kernels: 55.5 us -> 54.6 us
    pallas_call x1, Pallas kernels: 53.4 us -> 52.5 us  [shards(): pl.pallas_call(kernel, out_shape=shapes, in_specs=[anywhere] * 9, out_spe...]
where the time goes in v3:
time: 55.9 us; the launch traced here: 55.2 us
  Pallas kernels  54.6 us (98%)
  between operations  0.64 us (1%)
    pallas_call x1, Pallas kernels, shards(): pl.pallas_call(kernel, out_shape=shapes, in_specs=[anywhere] * 9, out_spe...  52.5 us
    pallas_call x1, Pallas kernels, shards(): pl.pallas_call(deliver, out_shape=shapes[:5] + [jax.ShapeDtypeStruct((HEA...  2.03 us

profile of v3, /device:TPU:1, one launch (start us, length us, event | category | flops | bytes accessed | tf_op | source)
XLA Modules:
  0.0 55.2 jit_solution(8505563336163717020)
XLA Ops:
  0.6 52.5 %shard_map.136 = (bf16[256,512]{1,0:T(8,128)(2,1)}, bf16[256,512]{1,0:T(8,128)(2,1)}, f32[8,384]{1,0:T(8,128)}, f32[8,128]{1,0:T(8,128)}, f32[1,512]{1,0:T(1,128)}, /*index=5*/f32[64,512]{1,0:T(8,128)}) custom-call(bf16[256,512]{1,0:T(8,128)(2,1)} %bitcast.7, bf16[256,512]{1,0:T(8,128)(2,1)} %teacher_hbm.1, bf16[512,1536]{1,0:T(8,128)(2,1)} %wqkv_hbm.1, ...), custom_call_target="tpu_custom_call" | custom-call | tf_op jit(solution)/shard_map/pallas_call | solution.py:488
  53.2 2.0 %shard_map.137 = (bf16[256,512]{1,0:T(8,128)(2,1)}, bf16[256,512]{1,0:T(8,128)(2,1)}, f32[8,384]{1,0:T(8,128)}, f32[8,128]{1,0:T(8,128)}, f32[1,512]{1,0:T(1,128)}, /*index=5*/f32[512,64]{1,0:T(8,128)}) custom-call(bf16[256,512]{1,0:T(8,128)(2,1)} %get-tuple-element.18.refs_0_, bf16[256,512]{1,0:T(8,128)(2,1)} %get-tuple-element.19.refs_1_, ...), custom_call_target="tpu_custom_call" | custom-call | tf_op jit(solution)/shard_map/pallas_call | solution.py:501

commit v4 on v3

--- a/solution.py
+++ b/solution.py
@@ -199,6 +199,9 @@
     normalise(2, xh[1])
     keys_values(2)
 
+    def column(row):
+        return jnp.broadcast_to(row, (8, HALF)).T[:, :1]
+
     for b in range(ROWS):
         tops = [peak[b, :, lanes] for lanes in groups]
         score(b, (0, 1, 2), tops)
@@ -209,14 +212,14 @@
             for s in range(SLOTS):
                 piece = jnp.exp(sref[b, s * PIX:(s + 1) * PIX, lanes] - top)
                 sref[b, s * PIX:(s + 1) * PIX, lanes] = piece
+                pb[b, s, :, lanes] = piece.astype(BF16)
                 total = piece if total is None else total + piece
             share = 1.0 / jnp.sum(total, axis=0, keepdims=True)
             rinv[b, :, lanes] = share
-            for s in range(SLOTS):
-                piece = sref[b, s * PIX:(s + 1) * PIX, lanes] * share
-                pb[b, s, :, lanes] = piece.astype(BF16)
             probs = pb[b, 0:SLOTS, :, lanes].reshape(SLOTS * PIX, HALF)
-            mixed[b * PIX:(b + 1) * PIX, lanes] = diagonal(mm(probs, vg[b, :, lanes], TN)).astype(BF16)
+            mixed[b * PIX:(b + 1) * PIX, lanes] = diagonal(
+                mm(probs, vg[b, :, lanes], TN) * column(share)
+            ).astype(BF16)
 
     load_out.wait()
     load_teacher.wait()
@@ -262,18 +265,18 @@
     dbias = None
     for b in range(ROWS):
         for g, lanes in enumerate(groups):
-            diag = block_diagonal(dmix[b * PIX:(b + 1) * PIX, lanes])
+            share = rinv[b, :, lanes]
+            rows = jnp.concatenate([dmix[b * PIX:(b + 1) * PIX, lanes].astype(F32)] * 4, axis=0)
+            diag = (rows * column(share)).astype(BF16) * same_head
             md[g, b * HALF:(b + 1) * HALF, :] = diag
             dprobs = mm(vg[b, :, lanes], diag, NT)
-            share = rinv[b, :, lanes]
             total = None
             for s in range(SLOTS):
                 piece = sref[b, s * PIX:(s + 1) * PIX, lanes] * dprobs[s * PIX:(s + 1) * PIX]
                 total = piece if total is None else total + piece
             delta = jnp.sum(total, axis=0, keepdims=True) * share
             for s in range(SLOTS):
-                piece = sref[b, s * PIX:(s + 1) * PIX, lanes] * share
-                piece = piece * (dprobs[s * PIX:(s + 1) * PIX] - delta)
+                piece = sref[b, s * PIX:(s + 1) * PIX, lanes] * (dprobs[s * PIX:(s + 1) * PIX] - delta)
                 dsb[b, s, :, lanes] = piece.astype(BF16)
             dscores = dsb[b, 0:SLOTS, :, lanes].reshape(SLOTS * PIX, HALF)
             dproj[HALF + b * PIX:HALF + (b + 1) * PIX, lanes] = (

time: 55.9 us -> 56.5 us (1.011)
  no operation moved by 1% of the time
where the time goes in v4:
time: 56.5 us; the launch traced here: 55.7 us
  Pallas kernels  55 us (97%)
  between operations  0.64 us (1%)
    pallas_call x1, Pallas kernels, shards(): pl.pallas_call(kernel, out_shape=shapes, in_specs=[anywhere] * 9, out_spe...  53 us
    pallas_call x1, Pallas kernels, shards(): pl.pallas_call(deliver, out_shape=shapes[:5] + [jax.ShapeDtypeStruct((HEA...  2.03 us

profile of v4, /device:TPU:1, one launch (start us, length us, event | category | flops | bytes accessed | tf_op | source)
XLA Modules:
  0.0 55.7 jit_solution(3749422563632297114)
XLA Ops:
  0.6 53.0 %shard_map.136 = (bf16[256,512]{1,0:T(8,128)(2,1)}, bf16[256,512]{1,0:T(8,128)(2,1)}, f32[8,384]{1,0:T(8,128)}, f32[8,128]{1,0:T(8,128)}, f32[1,512]{1,0:T(1,128)}, /*index=5*/f32[64,512]{1,0:T(8,128)}) custom-call(bf16[256,512]{1,0:T(8,128)(2,1)} %bitcast.7, bf16[256,512]{1,0:T(8,128)(2,1)} %teacher_hbm.1, bf16[512,1536]{1,0:T(8,128)(2,1)} %wqkv_hbm.1, ...), custom_call_target="tpu_custom_call" | custom-call | tf_op jit(solution)/shard_map/pallas_call | solution.py:491
  53.7 2.0 %shard_map.137 = (bf16[256,512]{1,0:T(8,128)(2,1)}, bf16[256,512]{1,0:T(8,128)(2,1)}, f32[8,384]{1,0:T(8,128)}, f32[8,128]{1,0:T(8,128)}, f32[1,512]{1,0:T(1,128)}, /*index=5*/f32[512,64]{1,0:T(8,128)}) custom-call(bf16[256,512]{1,0:T(8,128)(2,1)} %get-tuple-element.18.refs_0_, bf16[256,512]{1,0:T(8,128)(2,1)} %get-tuple-element.19.refs_1_, ...), custom_call_target="tpu_custom_call" | custom-call | tf_op jit(solution)/shard_map/pallas_call | solution.py:504
